TPU v7x, 256 devices: a whole 4x4x8 slice. The times are simulated.
256 devices in a mesh: gx: 32 (over z, y_lo, core), gy: 2 (over y_hi), gz: 4 (over x).
Axes of the slice: x: 4, y: 4 (y_hi: 2, y_lo: 2; y = y_hi * 2 + y_lo), z: 8, core: 2. Of those that a mesh axis runs over, the one named last changes fastest.
Arguments:
- jacobian: bfloat16 [32, 8, 12, 64, 1728], P('gx', 'gy', 'gz'), may hold values from -0.06 to 1.06
- columns: int32 [32, 8, 12, 27], P('gx', 'gy', 'gz'), may hold values from 0 to 26, as said below
- start: float32 [32, 8, 12, 64, 128], P('gx', 'gy', 'gz'), may hold values from -1800 to 1800
- velocity: float32 [32, 8, 12, 3, 16], P('gx', 'gy', 'gz'), may hold values from -6 to 6
- design: float32 [32, 8, 12, 16], P('gx', 'gy', 'gz'), may hold values from 0.05 to 1
- mask: int32 [32, 8, 12, 16], P('gx', 'gy', 'gz'), may hold values 0 or 1
Outputs:
- adjoint: float32 [32, 8, 12, 64, 128], P('gx', 'gy', 'gz')
- hessenberg: float32 [5, 128], replicated
- sensitivity: float32 [32, 8, 12, 16, 128], P('gx', 'gy', 'gz')
Inputs may be any that keep to these rules, and one draw needn't show every extreme that they name: `columns`: the 27 slots of each block row name every offset code once.
All inputs are finite; a program needn't handle non-finite values. No bound on the sum of `mask` on one device may be relied on, other than what follows from the above.
Results may differ from a plain program's by a relative error of at most 0.0057.
Values sent between devices are 32-bit elements; how exact they have to be, the bound alone decides.
A program may use at most 64 MiB of HBM per device.

v0:
```python
import jax
import jax.numpy as jnp
from jax import lax
from jax.sharding import PartitionSpec as P

epsilon = 1e-06


def passed_along(value, axis, steps):
    count = lax.axis_size(axis)
    initial, last = (max(0, -steps), min(count, count - steps))
    return lax.ppermute(value, axis, [(source, source + steps) for source in range(initial, last)])


def fold_along_x(pushed):
    from_below = passed_along(pushed[-1], "gx", 1)
    from_above = passed_along(pushed[0], "gx", -1)
    inner = pushed[1:-1]
    inner = inner.at[0].add(from_below)
    return inner.at[-1].add(from_above)


def fold_along_y(pushed):
    from_below = passed_along(pushed[:, -1], "gy", 1)
    from_above = passed_along(pushed[:, 0], "gy", -1)
    inner = pushed[:, 1:-1]
    inner = inner.at[:, 0].add(from_below)
    return inner.at[:, -1].add(from_above)


def fold_along_z(pushed):
    from_below = passed_along(pushed[:, :, -1], "gz", 1)
    from_above = passed_along(pushed[:, :, 0], "gz", -1)
    inner = pushed[:, :, 1:-1]
    inner = inner.at[:, :, 0].add(from_below)
    return inner.at[:, :, -1].add(from_above)


def order_blocks(jacobian, columns):
    blocks_x, blocks_y, blocks_z = (columns.shape[0], columns.shape[1], columns.shape[2])
    slots = columns.shape[3]
    width = jacobian.shape[3]
    order_ids = jnp.arange(slots, dtype=jnp.int32)
    hits = columns[:, :, :, None, :] == order_ids[:, None]
    slot_index = jnp.sum(jnp.where(hits, order_ids, 0), axis=-1)
    blocks = jacobian.reshape(blocks_x, blocks_y, blocks_z, width, slots, width)
    picked = jnp.take_along_axis(blocks, slot_index[:, :, :, None, :, None], axis=4)
    return jnp.moveaxis(picked, 4, 3)


def transpose_apply(ordered, field):
    blocks_x, blocks_y, blocks_z = (field.shape[0], field.shape[1], field.shape[2])
    field_low = field.astype(jnp.bfloat16)
    pushed = jnp.zeros(
        (blocks_x + 2, blocks_y + 2, blocks_z + 2, field.shape[3], field.shape[4]), jnp.float32
    )
    for offset in range(ordered.shape[3]):
        step_x = offset // 9 - 1
        step_y = offset // 3 % 3 - 1
        step_z = offset % 3 - 1
        product = jnp.einsum(
            "abcij,abcir->abcjr",
            ordered[:, :, :, offset],
            field_low,
            preferred_element_type=jnp.float32,
        )
        pushed = pushed.at[
            1 + step_x : 1 + step_x + blocks_x,
            1 + step_y : 1 + step_y + blocks_y,
            1 + step_z : 1 + step_z + blocks_z,
        ].add(product)
    return fold_along_z(fold_along_y(fold_along_x(pushed)))


def local_inner(left, right):
    return jnp.sum(left * right, axis=(0, 1, 2, 3))


def per_device(jacobian, columns, start, velocity, design, mask):
    devices_all = lax.axis_size("gx") * lax.axis_size("gy") * lax.axis_size("gz")
    entries = start.shape[0] * start.shape[1] * start.shape[2] * start.shape[3] * devices_all
    ordered = order_blocks(jacobian, columns)
    wide_raw = transpose_apply(ordered, start)
    start_sum = lax.psum(local_inner(start, start), ("gx", "gy", "gz"))
    scale = jnp.sqrt(start_sum / entries + epsilon)
    first = start / scale
    wide_one = wide_raw / scale
    coef_one = lax.psum(local_inner(wide_one, first), ("gx", "gy", "gz")) / entries
    rest_one = wide_one - coef_one * first
    norm_one = jnp.sqrt(
        lax.psum(local_inner(rest_one, rest_one), ("gx", "gy", "gz")) / entries + epsilon
    )
    second = rest_one / norm_one
    wide_two = transpose_apply(ordered, second)
    sum_two, sum_three = lax.psum(
        (local_inner(wide_two, first), local_inner(wide_two, second)), ("gx", "gy", "gz")
    )
    coef_two = sum_two / entries
    coef_three = sum_three / entries
    rest_two = wide_two - coef_two * first - coef_three * second
    norm_two = jnp.sqrt(
        lax.psum(local_inner(rest_two, rest_two), ("gx", "gy", "gz")) / entries + epsilon
    )
    adjoint = rest_two / norm_two
    hessenberg = jnp.stack([coef_one, norm_one, coef_two, coef_three, norm_two])
    cells = design.shape[3]
    shaped = adjoint.reshape(
        adjoint.shape[0],
        adjoint.shape[1],
        adjoint.shape[2],
        adjoint.shape[3] // cells,
        cells,
        adjoint.shape[4],
    )
    dotted = jnp.sum(velocity[..., None] * shaped[:, :, :, 0:3], axis=3)
    slope = -0.11 / ((0.1 + design) * (0.1 + design))
    sensitivity = (mask.astype(jnp.float32) * slope)[..., None] * dotted
    return (adjoint, hessenberg, sensitivity)


def solution(mesh):
    in_specs = (
        P("gx", "gy", "gz", None, None),
        P("gx", "gy", "gz", None),
        P("gx", "gy", "gz", None, None),
        P("gx", "gy", "gz", None, None),
        P("gx", "gy", "gz", None),
        P("gx", "gy", "gz", None),
    )
    out_specs = (P("gx", "gy", "gz", None, None), P(), P("gx", "gy", "gz", None, None))
    return jax.shard_map(
        per_device, mesh=mesh, in_specs=in_specs, out_specs=out_specs, check_vma=False
    )
```

profile of v0, /device:TPU:1, one launch (start us, length us, event | category | flops | bytes accessed | tf_op | source)
XLA Modules:
  0.0 537.4 jit_solution(3872559705358463508)
XLA Ops:
  0.6 2.2 select_reduce_fusion
  3.0 9.3 %reshape.3390 = bf16[4,3,64,27,64]{4,3,2,1,0:T(8,128)(2,1)} reshape(bf16[1,4,3,64,1728]{4,3,2,1,0:T(8,128)(2,1)} %param.138) | data formatting | bytes 5308416 | tf_op jit(solution)/shard_map/reshape | solution.py:46
  12.4 7.3 %copy.128 = bf16[4,3,64,27,64]{4,2,3,1,0:T(8,128)(2,1)} copy(bf16[4,3,64,27,64]{4,3,2,1,0:T(8,128)(2,1)} %reshape.3390) | data formatting | bytes 5308416 | tf_op jit(solution)/shard_map/reshape | solution.py:46
  19.7 9.6 %gather_fusion = bf16[324,64,64]{2,1,0:T(8,128)(2,1)} fusion(bf16[4,3,64,27,64]{4,2,3,1,0:T(8,128)(2,1)} %copy.128, s32[324]{0:T(512)S(1)} %reshape.3392), kind=kCustom, calls=%fused_computation | custom fusion | bytes 5312304 | tf_op jit(solution)/shard_map/jit(take_along_axis)/gather | solution.py:47
  29.3 8.1 %copy.129 = bf16[4,3,27,64,64]{3,4,1,0,2:T(8,128)(2,1)} copy(bf16[4,3,27,64,64]{4,3,2,1,0:T(8,128)(2,1)} %bitcast.580) | data formatting | bytes 5308416 | tf_op jit(solution)/shard_map/jit(take_along_axis)/gather | solution.py:47
  37.4 0.3 copy.126
  37.8 3.5 fusion
  41.5 0.3 scatter-add.206
  42.1 0.2 fusion.4
  42.7 0.9 fusion.181
  43.6 2.1 fusion.10
  50.1 0.2 slice_bitcast_fusion.3
  50.4 4.6 collective-permute-start
  55.0 1.9 collective-permute-start.1
  56.9 21.4 %collective-permute-done = f32[6,5,64,128]{3,2,1,0:T(8,128)S(1)} collective-permute-done((f32[6,5,64,128]{3,2,1,0:T(8,128)S(1)}, f32[6,5,64,128]{3,2,1,0:T(8,128)S(1)}, u32[]{:S(2)}, u32[]{:S(2)}) %collective-permute-start) | collective-permute-done | bytes 983072 | tf_op jit(solution)/shard_map/ppermute | solution.py:12
  78.3 0.2 fusion.106
  78.6 2.8 collective-permute-start.2
  81.4 80.5 %psum.42 = f32[128]{0:T(128)S(1)} all-reduce(f32[128]{0:T(128)S(1)} %get-tuple-element.827), channel_id=1, replica_groups=mesh['gx'=32,'gy'=2,'gz'=4] {'gx','gy','gz'}, use_global_device_ids=true, to_apply=%region_2.3 | all-reduce | flops 128 | bytes 1024 | tf_op jit(solution)/shard_map/psum | solution.py:84
  161.9 1.3 collective-permute-start.3
  163.2 7.1 %collective-permute-done.3 = f32[1,5,64,128]{3,2,1,0:T(8,128)S(1)} collective-permute-done((f32[1,5,64,128]{3,2,1,0:T(8,128)S(1)}, f32[1,5,64,128]{3,2,1,0:T(8,128)S(1)}, u32[]{:S(2)}, u32[]{:S(2)}) %collective-permute-start.3) | collective-permute-done | bytes 163872 | tf_op jit(solution)/shard_map/ppermute | solution.py:12
  170.4 2.9 collective-permute-start.4
  173.4 1.3 collective-permute-start.5
  174.7 0.5 collective-permute-done.4
  175.3 3.9 collective-permute-done.5
  179.3 74.9 %psum.43 = f32[128]{0:T(128)S(1)} all-reduce(f32[128]{0:T(128)S(1)} %multiply_reduce_fusion.4), channel_id=1, replica_groups=mesh['gx'=32,'gy'=2,'gz'=4] {'gx','gy','gz'}, use_global_device_ids=true, to_apply=%region_4.5 | all-reduce | flops 128 | bytes 1024 | tf_op jit(solution)/shard_map/psum | solution.py:88
  254.3 73.4 %psum.44 = f32[128]{0:T(128)S(1)} all-reduce(f32[128]{0:T(128)S(1)} %get-tuple-element.813), channel_id=1, replica_groups=mesh['gx'=32,'gy'=2,'gz'=4] {'gx','gy','gz'}, use_global_device_ids=true, to_apply=%region_6.7 | all-reduce | flops 128 | bytes 1024 | tf_op jit(solution)/shard_map/psum | solution.py:91
  327.8 1.3 convolution_bitcast_fusion.26
  329.1 0.3 scatter-add.259
  329.4 1.1 fusion.54
  330.6 1.1 fusion.56
  331.7 1.1 fusion.58
  332.9 0.2 fusion.60
  333.1 2.1 fusion.62
  335.2 0.2 fusion.64
  335.4 0.2 fusion.66
  335.6 0.2 fusion.68
  336.1 0.2 fusion.72
  336.3 0.2 fusion.74
  336.5 0.2 fusion.76
  336.7 0.2 fusion.78
  336.9 0.2 fusion.80
  337.1 0.2 fusion.82
  337.3 0.2 fusion.84
  337.5 0.2 fusion.86
  337.8 0.2 fusion.88
  338.0 0.2 fusion.90
  339.7 0.2 slice_bitcast_fusion.1
  339.9 3.5 collective-permute-start.6
  343.4 1.9 collective-permute-start.7
  345.3 21.4 %collective-permute-done.6 = f32[6,5,64,128]{3,2,1,0:T(8,128)S(1)} collective-permute-done((f32[6,5,64,128]{3,2,1,0:T(8,128)S(1)}, f32[6,5,64,128]{3,2,1,0:T(8,128)S(1)}, u32[]{:S(2)}, u32[]{:S(2)}) %collective-permute-start.6) | collective-permute-done | bytes 983072 | tf_op jit(solution)/shard_map/ppermute | solution.py:12
  366.7 0.3 fusion.105
  367.0 4.4 collective-permute-start.8
  371.5 1.3 collective-permute-start.9
  372.8 0.9 collective-permute-done.8
  373.7 5.3 collective-permute-done.9
  379.1 1.3 collective-permute-start.10
  380.5 1.3 collective-permute-start.11
  381.8 0.5 collective-permute-done.10
  382.4 3.8 collective-permute-done.11
  386.4 75.8 %all-reduce.2 = (f32[128]{0:T(128)S(1)}, f32[128]{0:T(128)S(1)}) all-reduce(f32[128]{0:T(128)S(1)} %get-tuple-element.808, f32[128]{0:T(128)S(1)} %get-tuple-element.807), channel_id=1, replica_groups=mesh['gx'=32,'gy'=2,'gz'=4] {'gx','gy','gz'}, use_global_device_ids=true, to_apply=%region_10.11 | all-reduce | flops 256 | bytes 2048 | tf_op jit(solution)/shard_map/psum | solution.py:95
  462.3 72.7 %psum.47 = f32[128]{0:T(128)S(1)} all-reduce(f32[128]{0:T(128)S(1)} %get-tuple-element.811), channel_id=1, replica_groups=mesh['gx'=32,'gy'=2,'gz'=4] {'gx','gy','gz'}, use_global_device_ids=true, to_apply=%region_12.13 | all-reduce | flops 128 | bytes 1024 | tf_op jit(solution)/shard_map/psum | solution.py:102
  535.1 0.8 copy.164
  536.1 0.6 copy.165
  536.8 0.6 stack.23
  (90 shorter events, 8.5 us)
Async XLA Ops:
  29.3 8.4 %copy-start.1 = (f32[1,4,3,64,128]{4,3,2,1,0:T(8,128)S(1)}, f32[1,4,3,64,128]{4,3,2,1,0:T(8,128)}, u32[]{:S(2)}) copy-start(f32[1,4,3,64,128]{4,3,2,1,0:T(8,128)} %param.140) | copy-start | bytes 1179652
  41.3 8.6 %copy-start = (bf16[1,4,3,27,64,64]{4,5,2,1,3,0:T(8,128)(2,1)}, bf16[1,4,3,27,64,64]{4,5,2,1,3,0:T(8,128)(2,1)S(1)}, u32[]{:S(2)}) copy-start(bf16[1,4,3,27,64,64]{4,5,2,1,3,0:T(8,128)(2,1)S(1)} %fusion) | copy-start | bytes 7962628
  50.4 27.9 %collective-permute-start = (f32[6,5,64,128]{3,2,1,0:T(8,128)S(1)}, f32[6,5,64,128]{3,2,1,0:T(8,128)S(1)}, u32[]{:S(2)}, u32[]{:S(2)}) collective-permute-start(f32[6,5,64,128]{3,2,1,0:T(8,128)S(1)} %get-tuple-element.817), channel_id=1, source_target_pairs={{0,8},{8,16},{16,24},{24,32},{32,40},{40,48},{48,56},{56,64},{64,7... | collective-permute-start | bytes 2949128 | tf_op jit(solution)/shard_map/ppermute | solution.py:12
  55.0 23.3 %collective-permute-start.1 = (f32[6,5,64,128]{3,2,1,0:T(8,128)S(1)}, f32[6,5,64,128]{3,2,1,0:T(8,128)S(1)}, u32[]{:S(2)}, u32[]{:S(2)}) collective-permute-start(f32[6,5,64,128]{3,2,1,0:T(8,128)S(1)} %get-tuple-element.818), channel_id=1, source_target_pairs={{8,0},{16,8},{24,16},{32,24},{40,32},{48,40},{56,48},{64,56},{72,6... | collective-permute-start | bytes 2949128 | tf_op jit(solution)/shard_map/ppermute | solution.py:12
  78.6 84.6 %collective-permute-start.2 = (f32[1,5,64,128]{3,2,1,0:T(8,128)S(1)}, f32[1,5,64,128]{3,2,1,0:T(8,128)S(1)}, u32[]{:S(2)}, u32[]{:S(2)}) collective-permute-start(f32[1,5,64,128]{3,2,1,0:T(8,128)S(1)} %get-tuple-element.822), channel_id=1, source_target_pairs={{0,4},{1,5},{2,6},{3,7},{8,12},{9,13},{10,14},{11,15},{16,20},{17,... | collective-permute-start | bytes 491528 | tf_op jit(solution)/shard_map/ppermute | solution.py:12
  161.9 8.5 %collective-permute-start.3 = (f32[1,5,64,128]{3,2,1,0:T(8,128)S(1)}, f32[1,5,64,128]{3,2,1,0:T(8,128)S(1)}, u32[]{:S(2)}, u32[]{:S(2)}) collective-permute-start(f32[1,5,64,128]{3,2,1,0:T(8,128)S(1)} %get-tuple-element.821), channel_id=1, source_target_pairs={{4,0},{5,1},{6,2},{7,3},{12,8},{13,9},{14,10},{15,11},{20,16},{21,... | collective-permute-start | bytes 491528 | tf_op jit(solution)/shard_map/ppermute | solution.py:12
  163.2 169.6 %slice-start = ((s8[5308416]{0:T(1024)(128)(4,1)}), s8[1114112]{0:T(1024)(128)(4,1)S(1)}, s32[]{:S(2)}) async-start(s8[5308416]{0:T(1024)(128)(4,1)} %bitcast.578), calls=%async_computation | async-start | bytes 2228224
  170.4 4.8 collective-permute-start.4
  173.4 5.7 %collective-permute-start.5 = (f32[1,4,64,128]{3,2,1,0:T(8,128)S(1)}, f32[1,4,64,128]{3,2,1,0:T(8,128)S(1)}, u32[]{:S(2)}, u32[]{:S(2)}) collective-permute-start(f32[1,4,64,128]{3,2,1,0:T(8,128)S(1)} %get-tuple-element.825), channel_id=1, source_target_pairs={{1,0},{2,1},{3,2},{5,4},{6,5},{7,6},{9,8},{10,9},{11,10},{13,12},{... | collective-permute-start | bytes 393224 | tf_op jit(solution)/shard_map/ppermute | solution.py:12
  327.8 5.0 slice-start.1
  339.9 31.5 %copy-start.2 = (f32[1,4,3,3,16]{4,1,3,2,0:T(4,128)S(1)}, f32[1,4,3,3,16]{4,1,3,2,0:T(4,128)}, u32[]{:S(2)}) copy-start(f32[1,4,3,3,16]{4,1,3,2,0:T(4,128)} %param.141) | copy-start | bytes 6916
  339.9 26.8 %collective-permute-start.6 = (f32[6,5,64,128]{3,2,1,0:T(8,128)S(1)}, f32[6,5,64,128]{3,2,1,0:T(8,128)S(1)}, u32[]{:S(2)}, u32[]{:S(2)}) collective-permute-start(f32[6,5,64,128]{3,2,1,0:T(8,128)S(1)} %get-tuple-element.815), channel_id=1, source_target_pairs={{0,8},{8,16},{16,24},{24,32},{32,40},{40,48},{48,56},{56,64},{64,7... | collective-permute-start | bytes 2949128 | tf_op jit(solution)/shard_map/ppermute | solution.py:12
  343.4 23.3 %collective-permute-start.7 = (f32[6,5,64,128]{3,2,1,0:T(8,128)S(1)}, f32[6,5,64,128]{3,2,1,0:T(8,128)S(1)}, u32[]{:S(2)}, u32[]{:S(2)}) collective-permute-start(f32[6,5,64,128]{3,2,1,0:T(8,128)S(1)} %get-tuple-element.816), channel_id=1, source_target_pairs={{8,0},{16,8},{24,16},{32,24},{40,32},{48,40},{56,48},{64,56},{72,6... | collective-permute-start | bytes 2949128 | tf_op jit(solution)/shard_map/ppermute | solution.py:12
  367.0 13.4 %copy-start.3 = (f32[1,4,3,16]{3,1,2,0:T(4,128)S(1)}, f32[1,4,3,16]{3,1,2,0:T(4,128)}, u32[]{:S(2)}) copy-start(f32[1,4,3,16]{3,1,2,0:T(4,128)} %param.142) | copy-start | bytes 2308
  367.0 13.4 %copy-start.4 = (s32[1,4,3,16]{3,1,2,0:T(4,128)S(1)}, s32[1,4,3,16]{3,1,2,0:T(4,128)}, u32[]{:S(2)}) copy-start(s32[1,4,3,16]{3,1,2,0:T(4,128)} %param.143) | copy-start | bytes 2308
  367.0 6.6 %collective-permute-start.8 = (f32[1,5,64,128]{3,2,1,0:T(8,128)S(1)}, f32[1,5,64,128]{3,2,1,0:T(8,128)S(1)}, u32[]{:S(2)}, u32[]{:S(2)}) collective-permute-start(f32[1,5,64,128]{3,2,1,0:T(8,128)S(1)} %get-tuple-element.820), channel_id=1, source_target_pairs={{0,4},{1,5},{2,6},{3,7},{8,12},{9,13},{10,14},{11,15},{16,20},{17,... | collective-permute-start | bytes 491528 | tf_op jit(solution)/shard_map/ppermute | solution.py:12
  371.5 7.6 %collective-permute-start.9 = (f32[1,5,64,128]{3,2,1,0:T(8,128)S(1)}, f32[1,5,64,128]{3,2,1,0:T(8,128)S(1)}, u32[]{:S(2)}, u32[]{:S(2)}) collective-permute-start(f32[1,5,64,128]{3,2,1,0:T(8,128)S(1)} %get-tuple-element.819), channel_id=1, source_target_pairs={{4,0},{5,1},{6,2},{7,3},{12,8},{13,9},{14,10},{15,11},{20,16},{21,... | collective-permute-start | bytes 491528 | tf_op jit(solution)/shard_map/ppermute | solution.py:12
  379.1 3.2 collective-permute-start.10
  380.5 5.7 %collective-permute-start.11 = (f32[1,4,64,128]{3,2,1,0:T(8,128)S(1)}, f32[1,4,64,128]{3,2,1,0:T(8,128)S(1)}, u32[]{:S(2)}, u32[]{:S(2)}) collective-permute-start(f32[1,4,64,128]{3,2,1,0:T(8,128)S(1)} %get-tuple-element.823), channel_id=1, source_target_pairs={{1,0},{2,1},{3,2},{5,4},{6,5},{7,6},{9,8},{10,9},{11,10},{13,12},{... | collective-permute-start | bytes 393224 | tf_op jit(solution)/shard_map/ppermute | solution.py:12
where the time goes:
time: 539 us; the launch traced here: 537 us
  blocking collectives  377 us (70%)
  waiting for transfers between devices  64.8 us (12%)
  local copies, waits for them, and re-layouts  39.2 us (7%)
  starting transfers between devices  28.4 us (5%)
  matrix products  18.6 us (3%)
  other arithmetic  7.46 us (1%)
    psum x1, blocking collectives, per_device(): start_sum = lax.psum(local_inner(start, start), ('gx', 'gy', 'gz'))  80.5 us
    psum x1, blocking collectives, per_device(): lax.psum((local_inner(wide_two, first), local_inner(wide_two, second)), (...  75.8 us
    psum x1, blocking collectives, per_device(): lax.psum(local_inner(wide_one, first), ('gx', 'gy', 'gz')) / entries  74.9 us
    psum x1, blocking collectives, per_device(): lax.psum(local_inner(rest_one, rest_one), ('gx', 'gy', 'gz')) / entries  73.4 us
    psum x1, blocking collectives, per_device(): lax.psum(local_inner(rest_two, rest_two), ('gx', 'gy', 'gz')) / entries  72.7 us
    ppermute x12, waiting for transfers between devices, passed_along(): lax.ppermute(value, axis, [(source, source + steps) for source in range(i...  64.8 us
    ppermute x12, starting transfers between devices, passed_along(): lax.ppermute(value, axis, [(source, source + steps) for source in range(i...  28.4 us
    dot_general x54, matrix products, transpose_apply(): jnp.einsum('abcij,abcir->abcjr', ordered[:, :, :, offset], field_low, pre...  18.6 us
  transfers between devices with their start and end apart: 12, of which 9 were waited for; matrix products, arithmetic and copies ran while one was open for 0% of the time, Pallas kernels for 0%

commit v1 on v0

v1 whole, which is shorter than its diff:
```python
import functools

import jax
import jax.numpy as jnp
from jax import lax
from jax.experimental import pallas as pl
from jax.experimental.pallas import tpu as pltpu
from jax.sharding import PartitionSpec as P

MESH = pl.DeviceIdType.MESH
epsilon = 1e-06
SLOTS = 27
WIDTH = 64
RHS = 128
ROWS_Y = 4
ROWS_Z = 3
TILE_SLOTS = 9
UP, DOWN = 0, 1


def divided(value, by):
    safe = by > 0
    return jnp.where(safe, value / jnp.where(safe, by, 1.0), 0.0)


def fitted(g11, g12, g22, a1, a2):
    det = g11 * g22 - g12 * g12
    good = det > 1e-4 * g11 * g22
    c2 = jnp.where(good, (g11 * a2 - g12 * a1) / jnp.where(good, det, 1.0), 0.0)
    return divided(a1 - g12 * c2, g11), c2


def total(value):
    return jnp.sum(value, axis=0)


def merged_one(g, c, r, e):
    whole = total(g)
    inner = total(g * c + e)
    centre = divided(inner, whole)
    d = c - centre
    return whole, centre, total(r + d * (2.0 * e + d * g)), total(e + d * g), inner


def merged_two(g11, g12, g22, c1, c2, r, e1, e2):
    w11, w12, w22 = total(g11), total(g12), total(g22)
    a1 = total(g11 * c1 + g12 * c2 + e1)
    a2 = total(g12 * c1 + g22 * c2 + e2)
    k1, k2 = fitted(w11, w12, w22, a1, a2)
    d1, d2 = c1 - k1, c2 - k2
    p1 = d1 * g11 + d2 * g12
    p2 = d1 * g12 + d2 * g22
    rest = total(r + d1 * (2.0 * e1 + p1) + d2 * (2.0 * e2 + p2))
    return w11, w12, w22, k1, k2, rest, total(e1 + p1), total(e2 + p2), a1, a2


def rows_of(block):
    return [block[:, k : k + 1, :] for k in range(8)]


def kernel(
    nx, ny, nz, low_count,
    inv_ref, j_ref, start_ref,
    rest_ref, hess_ref,
    jv, jt, prod, push, zrecv, xrecv, yrecv, field, second, plane_buf, line_buf,
    jsem, ssem, zs, zr, xs, xr, ys, yr, gs, gr,
):
    gx = lax.axis_index("gx")
    gy = lax.axis_index("gy")
    gz = lax.axis_index("gz")
    entries = float(nx * ny * nz * ROWS_Y * ROWS_Z * WIDTH)

    field_copy = pltpu.make_async_copy(start_ref, field, ssem)
    field_copy.start()

    def j_copy(order, cz):
        return pltpu.make_async_copy(j_ref.at[:, cz], jv.at[cz], jsem.at[order])

    cz_order = (0, 2, 1)
    for order, cz in enumerate(cz_order):
        j_copy(order, cz).start()

    high_count = nx // low_count
    n1 = nz * low_count
    n2 = ny * high_count
    gx_low = lax.rem(gx, low_count)
    gx_high = gx // low_count
    me1 = gz * low_count + gx_low
    me2 = gy * high_count + gx_high

    def peer1(step):
        p = lax.rem(me1 + step, n1)
        return (gx_high * low_count + lax.rem(p, low_count), gy, p // low_count)

    def peer2(step):
        p = lax.rem(me2 + step, n2)
        return (lax.rem(p, high_count) * low_count + gx_low, p // high_count, gz)

    barrier = pltpu.get_barrier_semaphore()

    def greet(device):
        pl.semaphore_signal(barrier, inc=1, device_id=device, device_id_type=MESH)

    for step in range(1, n1):
        greet(peer1(step))
    for step in range(1, n2):
        greet(peer2(step))

    below_outside = jnp.logical_and(gx > 0, gx_low == 0)
    above_outside = jnp.logical_and(gx < nx - 1, gx_low == low_count - 1)

    @pl.when(below_outside)
    def _():
        greet((gx - 1, gy, gz))

    @pl.when(above_outside)
    def _():
        greet((gx + 1, gy, gz))

    greeted = (
        n1 - 1 + n2 - 1 + jnp.where(below_outside, 1, 0) + jnp.where(above_outside, 1, 0)
    )

    def met():
        pl.semaphore_wait(barrier, greeted)

    has_z = (gz < nz - 1, gz > 0)
    from_z = (gz > 0, gz < nz - 1)
    halo_row = jnp.where(gy == 0, ROWS_Y - 1, 0)
    halo_step = jnp.where(gy == 0, 2, 0)

    def z_copy(t, way, dx):
        to = gz + 1 if way == UP else gz - 1
        return pltpu.make_async_remote_copy(
            src_ref=push.at[t, dx, 4 if way == UP else 0],
            dst_ref=zrecv.at[t, way, dx],
            send_sem=zs.at[t, way, dx],
            recv_sem=zr.at[t, way, dx],
            device_id=(gx, gy, to),
            device_id_type=MESH,
        )

    def x_copy(t, way, z):
        to = gx + 1 if way == UP else gx - 1
        return pltpu.make_async_remote_copy(
            src_ref=push.at[t, 2 if way == UP else 0, z],
            dst_ref=xrecv.at[t, way, z - 1],
            send_sem=xs.at[t, way, z - 1],
            recv_sem=xr.at[t, way, z - 1],
            device_id=(to, gy, gz),
            device_id_type=MESH,
        )

    has_x = (gx < nx - 1, gx > 0)
    from_x = (gx > 0, gx < nx - 1)

    def y_copy(t, z):
        return pltpu.make_async_remote_copy(
            src_ref=push.at[t, 1, z, ROWS_Y],
            dst_ref=yrecv.at[t, z - 1],
            send_sem=ys.at[t, z - 1],
            recv_sem=yr.at[t, z - 1],
            device_id=(gx, 1 - gy, gz),
            device_id_type=MESH,
        )

    def product(b, cz, offset):
        slot = inv_ref[b * ROWS_Z + cz, offset]
        return prod[cz, b, slot]

    def gather_plane(t, dx, z):
        for y in range(ROWS_Y + 1):
            value = None
            for cz in range(max(0, z - 2), min(ROWS_Z - 1, z) + 1):
                oz = z - cz
                if y == ROWS_Y:
                    pairs = [(halo_row, halo_step)]
                else:
                    pairs = [
                        (b, y + 1 - b) for b in range(max(0, y - 1), min(ROWS_Y - 1, y + 1) + 1)
                    ]
                for b, oy in pairs:
                    term = product(b, cz, dx * 9 + oy * 3 + oz)
                    value = term if value is None else value + term
            push[t, dx, z, y] = value

    def multiply(t, cz):
        source = field if t == 0 else second
        for half in range(ROWS_Y // 2):
            q = cz * 2 + half
            if t == 0:
                for column in range(0, SLOTS * WIDTH, 128):
                    size = min(128, SLOTS * WIDTH - column)
                    both = jnp.concatenate(
                        [
                            jv[cz, 2 * half, :, column : column + size],
                            jv[cz, 2 * half + 1, :, column : column + size],
                        ],
                        axis=0,
                    )
                    jt[q, column : column + size, :] = both.T
            one = source[2 * half, cz].astype(jnp.bfloat16)
            two = source[2 * half + 1, cz].astype(jnp.bfloat16)
            none = jnp.zeros_like(one)
            weights = jnp.concatenate(
                [jnp.concatenate([one, none], axis=1), jnp.concatenate([none, two], axis=1)], axis=0
            )
            for slot in range(0, SLOTS, TILE_SLOTS):
                out = jnp.dot(
                    jt[q, slot * WIDTH : (slot + TILE_SLOTS) * WIDTH, :],
                    weights,
                    preferred_element_type=jnp.float32,
                )
                tile = (TILE_SLOTS, WIDTH, RHS)
                prod[cz, 2 * half, slot : slot + TILE_SLOTS] = out[:, :RHS].reshape(tile)
                prod[cz, 2 * half + 1, slot : slot + TILE_SLOTS] = out[:, RHS:].reshape(tile)

    def start_if(condition, copy):
        @pl.when(condition)
        def _():
            copy.start()

    def apply(t):
        for order, cz in enumerate(cz_order):
            if t == 0:
                if order == 0:
                    field_copy.wait()
                j_copy(order, cz).wait()
            multiply(t, cz)
            if t == 0 and order == 0:
                met()
            if cz != 1:
                way, z = (DOWN, 0) if cz == 0 else (UP, 4)
                for dx in (0, 2):
                    gather_plane(t, dx, z)
                    start_if(has_z[way], z_copy(t, way, dx))
        for way, dx in ((UP, 2), (DOWN, 0)):
            gather_plane(t, dx, 2)
            start_if(has_x[way], x_copy(t, way, 2))
        for z in (3, 1):
            for way, dx in ((UP, 2), (DOWN, 0)):
                gather_plane(t, dx, z)
        for way, z in ((DOWN, 0), (UP, 4)):
            gather_plane(t, 1, z)
            start_if(has_z[way], z_copy(t, way, 1))
        for z in (2, 3, 1):
            gather_plane(t, 1, z)
        for way, z in ((DOWN, 3), (UP, 1)):
            for x_way, dx in ((DOWN, 0), (UP, 2)):

                @pl.when(from_z[way])
                def _():
                    z_copy(t, way, dx).wait_recv()
                    push[t, dx, z] = push[t, dx, z] + zrecv[t, way, dx]

                start_if(has_x[x_way], x_copy(t, x_way, z))
        for way, z in ((DOWN, 3), (UP, 1)):

            @pl.when(from_z[way])
            def _():
                z_copy(t, way, 1).wait_recv()
                push[t, 1, z] = push[t, 1, z] + zrecv[t, way, 1]

        for z in (2, 3, 1):
            for way in (UP, DOWN):

                @pl.when(from_x[way])
                def _():
                    x_copy(t, way, z).wait_recv()
                    push[t, 1, z] = push[t, 1, z] + xrecv[t, way, z - 1]

            y_copy(t, z).start()
        for z in (2, 3, 1):
            y_copy(t, z).wait_recv()
            push[t, 1, z, halo_row] = push[t, 1, z, halo_row] + yrecv[t, z - 1]

    def finish(t):
        for way in (UP, DOWN):

            @pl.when(has_z[way])
            def _():
                for dx in range(3):
                    z_copy(t, way, dx).wait_send()

            @pl.when(has_x[way])
            def _():
                for z in range(1, 4):
                    x_copy(t, way, z).wait_send()

        for z in range(1, 4):
            y_copy(t, z).wait_send()

    def wide(t, b, cz):
        return push[t, 1, cz + 1, b]

    cells = [(b, cz) for b in range(ROWS_Y) for cz in range(ROWS_Z)]

    def summed(terms):
        acc = None
        for term in terms:
            acc = term if acc is None else acc + term
        return jnp.sum(acc, axis=0, keepdims=True)

    def exchange(buf, t, stage, me, peer, count):
        def copy(step):
            return pltpu.make_async_remote_copy(
                src_ref=buf.at[t, me],
                dst_ref=buf.at[t, me],
                send_sem=gs.at[t, stage],
                recv_sem=gr.at[t, stage],
                device_id=peer(step),
                device_id_type=MESH,
            )

        for step in range(1, count):
            copy(step).start()
        every = pltpu.make_async_remote_copy(
            src_ref=buf.at[t, pl.ds(0, count - 1)],
            dst_ref=buf.at[t, pl.ds(0, count - 1)],
            send_sem=gs.at[t, stage],
            recv_sem=gr.at[t, stage],
            device_id=peer(1),
            device_id_type=MESH,
        )
        every.wait_send()
        every.wait_recv()
        return rows_of(buf[t])

    def put(buf, t, me, rows):
        blank = [jnp.zeros((1, RHS), jnp.float32)] * (8 - len(rows))
        buf[t, me] = jnp.concatenate(list(rows) + blank, axis=0)

    apply(0)
    g = summed(field[b, cz] * field[b, cz] for b, cz in cells)
    a = summed(wide(0, b, cz) * field[b, cz] for b, cz in cells)
    c = divided(a, g)
    r = summed((wide(0, b, cz) - c * field[b, cz]) ** 2 for b, cz in cells)
    e = summed((wide(0, b, cz) - c * field[b, cz]) * field[b, cz] for b, cz in cells)
    put(plane_buf, 0, me1, (g, c, r, e))
    rows = exchange(plane_buf, 0, 0, me1, peer1, n1)
    put(line_buf, 0, me2, merged_one(*rows[:4])[:4])
    rows = exchange(line_buf, 0, 1, me2, peer2, n2)
    g, c, r, e, a = merged_one(*rows[:4])
    scale_square = g / entries + epsilon
    scale = jnp.sqrt(scale_square)
    coef_one = a / entries / scale_square
    d = c - coef_one
    r = jnp.maximum(r + d * (2.0 * e + d * g), 0.0)
    norm_one = jnp.sqrt(r / entries / scale_square + epsilon)
    inv_scale = 1.0 / scale
    inv_second = 1.0 / norm_one
    for b, cz in cells:
        first = field[b, cz] * inv_scale
        second[b, cz] = (wide(0, b, cz) * inv_scale - coef_one * first) * inv_second
        field[b, cz] = first

    apply(1)
    g11 = summed(field[b, cz] * field[b, cz] for b, cz in cells)
    g12 = summed(field[b, cz] * second[b, cz] for b, cz in cells)
    g22 = summed(second[b, cz] * second[b, cz] for b, cz in cells)
    a1 = summed(wide(1, b, cz) * field[b, cz] for b, cz in cells)
    a2 = summed(wide(1, b, cz) * second[b, cz] for b, cz in cells)
    c1, c2 = fitted(g11, g12, g22, a1, a2)
    for b, cz in cells:
        rest_ref[b, cz] = wide(1, b, cz) - c1 * field[b, cz] - c2 * second[b, cz]
    r = summed(rest_ref[b, cz] * rest_ref[b, cz] for b, cz in cells)
    e1 = summed(rest_ref[b, cz] * field[b, cz] for b, cz in cells)
    e2 = summed(rest_ref[b, cz] * second[b, cz] for b, cz in cells)
    put(plane_buf, 1, me1, (g11, g12, g22, c1, c2, r, e1, e2))
    rows = exchange(plane_buf, 1, 0, me1, peer1, n1)
    put(line_buf, 1, me2, merged_two(*rows)[:8])
    rows = exchange(line_buf, 1, 1, me2, peer2, n2)
    g11, g12, g22, c1, c2, r, e1, e2, a1, a2 = merged_two(*rows)
    coef_two = a1 / entries
    coef_three = a2 / entries
    d1, d2 = c1 - coef_two, c2 - coef_three
    p1 = d1 * g11 + d2 * g12
    p2 = d1 * g12 + d2 * g22
    r = jnp.maximum(r + d1 * (2.0 * e1 + p1) + d2 * (2.0 * e2 + p2), 0.0)
    norm_two = jnp.sqrt(r / entries + epsilon)
    for b, cz in cells:
        rest_ref[b, cz] = wide(1, b, cz) - coef_two * field[b, cz] - coef_three * second[b, cz]
    hess_ref[...] = jnp.concatenate(
        [coef_one, norm_one, coef_two, coef_three, norm_two, norm_two, norm_two, norm_two], axis=0
    )
    finish(0)
    finish(1)


def per_device(nx, ny, nz, jacobian, columns, start, velocity, design, mask):
    low_count = min(4, nx)
    n1 = nz * low_count
    n2 = ny * (nx // low_count)
    flat = columns.reshape(ROWS_Y * ROWS_Z, SLOTS)
    order_ids = jnp.arange(SLOTS, dtype=jnp.int32)
    hits = flat[:, None, :] == order_ids[:, None]
    inverse = jnp.sum(jnp.where(hits, order_ids, 0), axis=-1)
    block = (WIDTH, RHS)
    f32 = jnp.float32
    rest, hess = pl.pallas_call(
        functools.partial(kernel, nx, ny, nz, low_count),
        out_shape=(
            jax.ShapeDtypeStruct((ROWS_Y, ROWS_Z) + block, f32),
            jax.ShapeDtypeStruct((8, RHS), f32),
        ),
        in_specs=[
            pl.BlockSpec(memory_space=pltpu.SMEM),
            pl.BlockSpec(memory_space=pl.ANY),
            pl.BlockSpec(memory_space=pl.ANY),
        ],
        out_specs=(
            pl.BlockSpec(memory_space=pltpu.VMEM),
            pl.BlockSpec(memory_space=pltpu.VMEM),
        ),
        scratch_shapes=[
            pltpu.VMEM((ROWS_Z, ROWS_Y, WIDTH, SLOTS * WIDTH), jnp.bfloat16),
            pltpu.VMEM((ROWS_Z * ROWS_Y // 2, SLOTS * WIDTH, 2 * WIDTH), jnp.bfloat16),
            pltpu.VMEM((ROWS_Z, ROWS_Y, SLOTS) + block, f32),
            pltpu.VMEM((2, 3, ROWS_Z + 2, ROWS_Y + 1) + block, f32),
            pltpu.VMEM((2, 2, 3, ROWS_Y + 1) + block, f32),
            pltpu.VMEM((2, 2, ROWS_Z, ROWS_Y + 1) + block, f32),
            pltpu.VMEM((2, ROWS_Z) + block, f32),
            pltpu.VMEM((ROWS_Y, ROWS_Z) + block, f32),
            pltpu.VMEM((ROWS_Y, ROWS_Z) + block, f32),
            pltpu.VMEM((2, n1, 8, RHS), f32),
            pltpu.VMEM((2, n2, 8, RHS), f32),
            pltpu.SemaphoreType.DMA((3,)),
            pltpu.SemaphoreType.DMA,
            pltpu.SemaphoreType.DMA((2, 2, 3)),
            pltpu.SemaphoreType.DMA((2, 2, 3)),
            pltpu.SemaphoreType.DMA((2, 2, 3)),
            pltpu.SemaphoreType.DMA((2, 2, 3)),
            pltpu.SemaphoreType.DMA((2, 3)),
            pltpu.SemaphoreType.DMA((2, 3)),
            pltpu.SemaphoreType.DMA((2, 2)),
            pltpu.SemaphoreType.DMA((2, 2)),
        ],
        compiler_params=pltpu.CompilerParams(
            collective_id=0, has_side_effects=True, vmem_limit_bytes=48 * 1024 * 1024
        ),
    )(
        inverse,
        jacobian.reshape(ROWS_Y, ROWS_Z, WIDTH, SLOTS * WIDTH),
        start.reshape((ROWS_Y, ROWS_Z) + block),
    )
    hessenberg = hess[:5]
    adjoint = (rest / hess[4]).reshape(start.shape)
    cells = design.shape[3]
    shaped = adjoint.reshape(adjoint.shape[:3] + (WIDTH // cells, cells, RHS))
    dotted = jnp.sum(velocity[..., None] * shaped[:, :, :, 0:3], axis=3)
    slope = -0.11 / ((0.1 + design) * (0.1 + design))
    sensitivity = (mask.astype(f32) * slope)[..., None] * dotted
    return (adjoint, hessenberg, sensitivity)


def solution(mesh):
    shape = mesh.shape
    in_specs = (
        P("gx", "gy", "gz", None, None),
        P("gx", "gy", "gz", None),
        P("gx", "gy", "gz", None, None),
        P("gx", "gy", "gz", None, None),
        P("gx", "gy", "gz", None),
        P("gx", "gy", "gz", None),
    )
    out_specs = (P("gx", "gy", "gz", None, None), P(), P("gx", "gy", "gz", None, None))
    return jax.shard_map(
        functools.partial(per_device, shape["gx"], shape["gy"], shape["gz"]),
        mesh=mesh,
        in_specs=in_specs,
        out_specs=out_specs,
        check_vma=False,
    )
```

time: 539 us -> 84.8 us (0.16)
  blocking collectives: 377 us -> 0 us
  Pallas kernels: 0 us -> 77.7 us
  waiting for transfers between devices: 64.8 us -> 0 us
  local copies, waits for them, and re-layouts: 39.2 us -> 4.12 us
  starting transfers between devices: 28.4 us -> 0 us
  matrix products: 18.6 us -> 0 us
  other arithmetic: 7.46 us -> 1.99 us
    psum x5 -> x0, blocking collectives: 377 us -> none  [the longest x1 80.5 us: per_device(): start_sum = lax.psum(local_inner(start, start), ('gx', 'gy', 'gz'))]
    pallas_call x0 -> x1, Pallas kernels: none -> 77.7 us  [per_device(): pl.pallas_call(functools.partial(kernel, nx, ny, nz, low_count), out_shap...]
    ppermute x12 -> x0, waiting for transfers between devices: 64.8 us -> none  [passed_along(): lax.ppermute(value, axis, [(source, source + steps) for source in range(i...]
    ppermute x12 -> x0, starting transfers between devices: 28.4 us -> none  [passed_along(): lax.ppermute(value, axis, [(source, source + steps) for source in range(i...]
    dot_general x54 -> x0, matrix products: 18.6 us -> none  [transpose_apply(): jnp.einsum('abcij,abcir->abcjr', ordered[:, :, :, offset], field_low, pre...]
    gather x4 -> x0, local copies, waits for them, and re-layouts: 17.9 us -> none  [order_blocks(): jnp.take_along_axis(blocks, slot_index[:, :, :, None, :, None], axis=4)]
    reshape x2 -> x0, local copies, waits for them, and re-layouts: 16.6 us -> none  [order_blocks(): blocks = jacobian.reshape(blocks_x, blocks_y, blocks_z, width, slots, width)]
  transfers between devices with their start and end apart: 12 -> 0, of which waited for: 9 -> 0; matrix products, arithmetic and copies ran while one was open for 0% -> 0% of each run, Pallas kernels for 0% -> 0%
where the time goes in v1:
time: 84.8 us; the launch traced here: 84.6 us
  Pallas kernels  77.7 us (92%)
  local copies, waits for them, and re-layouts  4.12 us (5%)
  other arithmetic  1.99 us (2%)
    pallas_call x1, Pallas kernels, per_device(): pl.pallas_call(functools.partial(kernel, nx, ny, nz, low_count), out_shap...  77.7 us
    unnamed x12, local copies, waits for them, and re-layouts  4.09 us

profile of v1, /device:TPU:1, one launch (start us, length us, event | category | flops | bytes accessed | tf_op | source)
XLA Modules:
  0.0 84.6 jit_solution(9626622666115281335)
XLA Ops:
  0.6 0.0 copy-start.2
  0.6 0.0 copy-start.3
  0.7 0.0 copy-start.4
  0.7 0.7 copy.14
  1.4 0.3 select_reduce_fusion.inv_ref
  1.7 0.0 copy-start
  1.7 1.8 %copy-done = bf16[1,4,3,64,1728]{4,3,2,1,0:T(8,128)(2,1)S(1)} copy-done((bf16[1,4,3,64,1728]{4,3,2,1,0:T(8,128)(2,1)S(1)}, bf16[1,4,3,64,1728]{4,3,2,1,0:T(8,128)(2,1)}, u32[]{:S(2)}) %copy-start) | copy-done | bytes 2654232
  3.5 0.0 copy-start.1
  3.5 1.0 %copy-done.1 = f32[1,4,3,64,128]{4,3,2,1,0:T(8,128)S(1)} copy-done((f32[1,4,3,64,128]{4,3,2,1,0:T(8,128)S(1)}, f32[1,4,3,64,128]{4,3,2,1,0:T(8,128)}, u32[]{:S(2)}) %copy-start.1) | copy-done | bytes 393240
  4.4 77.7 %shard_map.85 = (f32[4,3,64,128]{3,2,1,0:T(8,128)S(1)}, f32[8,128]{1,0:T(8,128)S(1)}) custom-call(s32[12,27]{1,0:T(8,128)S(1)} %select_reduce_fusion.inv_ref, bf16[4,3,64,1728]{3,2,1,0:T(8,128)(2,1)S(1)} %bitcast.13, f32[4,3,64,128]{3,2,1,0:T(8,128)S(1)} %bitcast.14), custom_call_target="tpu_custom_call" | custom-call | tf_op jit(solution)/shard_map/pallas_call | solution.py:400
  82.3 0.0 copy-done.2
  82.3 0.1 fusion
  82.4 0.0 copy-done.3
  82.4 0.0 copy-done.4
  82.5 0.7 bitcast_multiply_fusion
  83.2 0.8 fusion.2
  84.0 0.6 copy.18
  (6 shorter events, 0.1 us)
Async XLA Ops:
  0.6 81.6 %copy-start.2 = (f32[1,4,3,3,16]{4,1,3,2,0:T(4,128)S(1)}, f32[1,4,3,3,16]{4,1,3,2,0:T(4,128)}, u32[]{:S(2)}) copy-start(f32[1,4,3,3,16]{4,1,3,2,0:T(4,128)} %param.9) | copy-start | bytes 6916
  0.6 81.8 %copy-start.3 = (f32[1,4,3,16]{3,1,2,0:T(4,128)S(1)}, f32[1,4,3,16]{3,1,2,0:T(4,128)}, u32[]{:S(2)}) copy-start(f32[1,4,3,16]{3,1,2,0:T(4,128)} %param.10) | copy-start | bytes 2308
  0.7 81.8 %copy-start.4 = (s32[1,4,3,16]{3,1,2,0:T(4,128)S(1)}, s32[1,4,3,16]{3,1,2,0:T(4,128)}, u32[]{:S(2)}) copy-start(s32[1,4,3,16]{3,1,2,0:T(4,128)} %param.11) | copy-start | bytes 2308
  1.7 1.8 %copy-start = (bf16[1,4,3,64,1728]{4,3,2,1,0:T(8,128)(2,1)S(1)}, bf16[1,4,3,64,1728]{4,3,2,1,0:T(8,128)(2,1)}, u32[]{:S(2)}) copy-start(bf16[1,4,3,64,1728]{4,3,2,1,0:T(8,128)(2,1)} %param.6) | copy-start | bytes 7962628
  3.5 1.0 %copy-start.1 = (f32[1,4,3,64,128]{4,3,2,1,0:T(8,128)S(1)}, f32[1,4,3,64,128]{4,3,2,1,0:T(8,128)}, u32[]{:S(2)}) copy-start(f32[1,4,3,64,128]{4,3,2,1,0:T(8,128)} %param.8) | copy-start | bytes 1179652

commit v2 on v1

v2 whole, which is shorter than its diff:
```python
import functools

import jax
import jax.numpy as jnp
from jax import lax
from jax.experimental import pallas as pl
from jax.experimental.pallas import tpu as pltpu
from jax.sharding import PartitionSpec as P

MESH = pl.DeviceIdType.MESH
epsilon = 1e-06
SLOTS = 27
WIDTH = 64
RHS = 128
ROWS_Y = 4
ROWS_Z = 3
TILE_SLOTS = 9
UP, DOWN = 0, 1


def divided(value, by):
    safe = by > 0
    return jnp.where(safe, value / jnp.where(safe, by, 1.0), 0.0)


def fitted(g11, g12, g22, a1, a2):
    det = g11 * g22 - g12 * g12
    good = det > 1e-4 * g11 * g22
    c2 = jnp.where(good, (g11 * a2 - g12 * a1) / jnp.where(good, det, 1.0), 0.0)
    return divided(a1 - g12 * c2, g11), c2


def total(value):
    return jnp.sum(value, axis=0)


def merged_one(g, c, r, e):
    whole = total(g)
    inner = total(g * c + e)
    centre = divided(inner, whole)
    d = c - centre
    return whole, centre, total(r + d * (2.0 * e + d * g)), total(e + d * g), inner


def merged_two(g11, g12, g22, c1, c2, r, e1, e2):
    w11, w12, w22 = total(g11), total(g12), total(g22)
    a1 = total(g11 * c1 + g12 * c2 + e1)
    a2 = total(g12 * c1 + g22 * c2 + e2)
    k1, k2 = fitted(w11, w12, w22, a1, a2)
    d1, d2 = c1 - k1, c2 - k2
    p1 = d1 * g11 + d2 * g12
    p2 = d1 * g12 + d2 * g22
    rest = total(r + d1 * (2.0 * e1 + p1) + d2 * (2.0 * e2 + p2))
    return w11, w12, w22, k1, k2, rest, total(e1 + p1), total(e2 + p2), a1, a2


def rows_of(block):
    return [block[:, k : k + 1, :] for k in range(8)]


def kernel(
    nx, ny, nz,
    codes_ref, j_ref, start_ref,
    rest_ref, hess_ref,
    inv_vmem, inv_ref, jv, jt, prod, push, near_buf, z_buf, far_buf, corner_buf, y_buf, field, second, image, plane_buf, line_buf,
    isem, jsem, ssem, ns, nr, zs, zr, zos, zor, ms, mr, fs, fr, cs, cr, ys, yr, gs, gr,
):
    gx = lax.axis_index("gx")
    gy = lax.axis_index("gy")
    gz = lax.axis_index("gz")
    entries = float(nx * ny * nz * ROWS_Y * ROWS_Z * WIDTH)

    field_copy = pltpu.make_async_copy(start_ref, field, ssem)

    def j_copy(order, cz):
        return pltpu.make_async_copy(j_ref.at[:, cz], jv.at[cz], jsem.at[order])

    cz_order = (0, 2, 1)
    j_copy(0, 0).start()
    field_copy.start()
    j_copy(1, 2).start()
    j_copy(2, 1).start()

    layers = nx // 4
    layer = gx // 4
    low = lax.rem(gx // 2, 2)
    core = lax.rem(gx, 2)
    chip_y = gy * 2 + low
    chips_y = ny * 2

    def distance(step, size):
        return min(step, size - step)

    n1, me1 = chips_y * nz, chip_y * nz + gz
    n2, me2 = layers * 2, layer * 2 + core
    steps1 = sorted(
        ((dy, dz) for dy in range(chips_y) for dz in range(nz) if dy or dz),
        key=lambda o: (-distance(o[0], chips_y) - distance(o[1], nz), o),
    )
    steps2 = sorted(
        ((dl, dc) for dl in range(layers) for dc in range(2) if dl or dc),
        key=lambda o: (-distance(o[0], layers), o),
    )

    def peer1(step):
        y = lax.rem(chip_y + step[0], chips_y)
        return ((layer * 2 + lax.rem(y, 2)) * 2 + core, y // 2, lax.rem(gz + step[1], nz))

    def peer2(step):
        other = lax.rem(layer + step[0], layers)
        return ((other * 2 + low) * 2 + lax.rem(core + step[1], 2), gy, gz)

    far = core * 2
    near = 2 - far
    far_x = gx + far - 1
    has_far = jnp.logical_and(far_x >= 0, far_x < nx)
    far_device = (far_x, gy, gz)
    corner_device = (far_x, 1 - gy, gz)
    near_device = (gx + near - 1, gy, gz)
    side_device = (gx, 1 - gy, gz)
    has_z = (gz < nz - 1, gz > 0)
    from_z = (gz > 0, gz < nz - 1)
    halo_row = jnp.where(gy == 0, ROWS_Y - 1, 0)
    halo_step = jnp.where(gy == 0, 2, 0)

    barrier = pltpu.get_barrier_semaphore()

    def greet(device):
        pl.semaphore_signal(barrier, inc=1, device_id=device, device_id_type=MESH)

    for step in steps1:
        greet(peer1(step))
    for step in steps2:
        greet(peer2(step))

    @pl.when(has_far)
    def _():
        greet(far_device)
        greet(corner_device)

    greeted = n1 - 1 + n2 - 1 + jnp.where(has_far, 2, 0)

    codes = jnp.concatenate([codes_ref[cz] for cz in range(ROWS_Z)], axis=0)
    place = lax.broadcasted_iota(jnp.int32, codes.shape, 1)
    inverse = jnp.zeros_like(codes)
    for code in range(SLOTS):
        slot = jnp.max(jnp.where(codes == code, place, 0), axis=1, keepdims=True)
        inverse = jnp.where(place == code, slot, inverse)
    inv_vmem[...] = jnp.zeros_like(inv_vmem)
    inv_vmem[: ROWS_Y * ROWS_Z, :SLOTS] = inverse
    inv_copy = pltpu.make_async_copy(inv_vmem, inv_ref, isem)
    inv_copy.start()

    def send(source, target, send_sem, recv_sem, device):
        return pltpu.make_async_remote_copy(
            src_ref=source,
            dst_ref=target,
            send_sem=send_sem,
            recv_sem=recv_sem,
            device_id=device,
            device_id_type=MESH,
        )

    def near_copy(t, z):
        return send(push.at[t, near, z], near_buf.at[t, z], ns.at[t, z], nr.at[t, z], near_device)

    def z_device(way):
        return (gx, gy, gz + 1 if way == UP else gz - 1)

    def z_far_copy(t, way, y):
        return send(
            push.at[t, far, 4 if way == UP else 0, y],
            z_buf.at[t, way, 0, y],
            zs.at[t, way, y],
            zr.at[t, way, y],
            z_device(way),
        )

    def z_own_copy(t, way, part):
        rows = pl.ds(ROWS_Y, 1) if part == 0 else pl.ds(0, ROWS_Y)
        return send(
            push.at[t, 1, 4 if way == UP else 0, rows],
            z_buf.at[t, way, 1, rows],
            zos.at[t, way, part],
            zor.at[t, way, part],
            z_device(way),
        )

    def middle_copy(t):
        return send(
            push.at[t, far, 2, pl.ds(0, ROWS_Y)], far_buf.at[t, 1], ms.at[t], mr.at[t], far_device
        )

    def far_copy(t, z, y):
        return send(
            push.at[t, far, z, y],
            far_buf.at[t, z - 1, y],
            fs.at[t, z // 2, y],
            fr.at[t, z // 2, y],
            far_device,
        )

    def corner_copy(t):
        return send(
            push.at[t, far, pl.ds(1, ROWS_Z), ROWS_Y],
            corner_buf.at[t],
            cs.at[t],
            cr.at[t],
            corner_device,
        )

    def y_copy(t):
        return send(
            push.at[t, 1, pl.ds(1, ROWS_Z), ROWS_Y], y_buf.at[t], ys.at[t], yr.at[t], side_device
        )

    def gather_plane(t, dx, z):
        for y in range(ROWS_Y + 1):
            value = None
            for cz in range(max(0, z - 2), min(ROWS_Z - 1, z) + 1):
                oz = z - cz
                if y == ROWS_Y:
                    pairs = [(halo_row, halo_step)]
                else:
                    pairs = [
                        (b, y + 1 - b) for b in range(max(0, y - 1), min(ROWS_Y - 1, y + 1) + 1)
                    ]
                for b, oy in pairs:
                    term = prod[cz, b, inv_ref[cz * ROWS_Y + b, dx * 9 + oy * 3 + oz]]
                    value = term if value is None else value + term
            push[t, dx, z, y] = value

    def terms(value):
        high = value.astype(jnp.bfloat16)
        return high, (value - high.astype(jnp.float32)).astype(jnp.bfloat16)

    def multiply(t, cz):
        for half in range(ROWS_Y // 2):
            q = cz * 2 + half
            if t == 0:
                for column in range(0, SLOTS * WIDTH, 128):
                    size = min(128, SLOTS * WIDTH - column)
                    both = jnp.concatenate(
                        [
                            jv[cz, 2 * half, :, column : column + size],
                            jv[cz, 2 * half + 1, :, column : column + size],
                        ],
                        axis=0,
                    ).T
                    jt[q, column : column + size, :128] = both
                    jt[q, column : column + size, 128:] = both
            one = terms(source(t, 2 * half, cz))
            two = terms(source(t, 2 * half + 1, cz))
            none = jnp.zeros_like(one[0])
            weights = jnp.concatenate(
                [
                    jnp.concatenate(pair, axis=1)
                    for k in range(2)
                    for pair in ([one[k], none], [none, two[k]])
                ],
                axis=0,
            )
            for slot in range(0, SLOTS, TILE_SLOTS):
                out = jnp.dot(
                    jt[q, slot * WIDTH : (slot + TILE_SLOTS) * WIDTH, :],
                    weights,
                    preferred_element_type=jnp.float32,
                )
                tile = (TILE_SLOTS, WIDTH, RHS)
                prod[cz, 2 * half, slot : slot + TILE_SLOTS] = out[:, :RHS].reshape(tile)
                prod[cz, 2 * half + 1, slot : slot + TILE_SLOTS] = out[:, RHS:].reshape(tile)

    def wide(t, b, cz):
        return push[t, 1, cz + 1, b]

    def source(t, b, cz):
        return field[b, cz] if t == 0 else wide(0, b, cz)

    def apply(t, beside, later):
        waiting = []

        def out(action):
            if t == 0:
                waiting.append(action)
            else:
                action()

        def out_z_far(way):
            @pl.when(has_z[way])
            def _():
                for y in range(ROWS_Y + 1):
                    z_far_copy(t, way, y).start()

        def out_middle():
            @pl.when(has_far)
            def _():
                middle_copy(t).start()

        for order, cz in enumerate(cz_order):
            if t == 0:
                j_copy(order, cz).wait()
                if order == 0:
                    field_copy.wait()
            multiply(t, cz)
            if t == 0 and order == 0:
                inv_copy.wait()
            if cz == 1:
                continue
            way, z = (DOWN, 0) if cz == 0 else (UP, 4)
            gather_plane(t, far, z)
            out(functools.partial(out_z_far, way))

        gather_plane(t, far, 2)
        out(out_middle)
        for z in (0, 4, 2, 3, 1):
            gather_plane(t, near, z)
            out(near_copy(t, z).start)
        gather_plane(t, far, 3)
        gather_plane(t, far, 1)
        for z in (0, 4, 2, 3, 1):
            gather_plane(t, 1, z)
        if t == 0:
            pl.semaphore_wait(barrier, greeted)
        for action in waiting:
            action()
        for way, z in ((DOWN, 0), (UP, 4)):
            near_copy(t, z).wait_recv()
            push[t, 1, z] = push[t, 1, z] + near_buf[t, z]

            @pl.when(has_z[way])
            def _():
                z_own_copy(t, way, 0).start()
                z_own_copy(t, way, 1).start()

        for z in (2, 3, 1):
            near_copy(t, z).wait_recv()
            push[t, 1, z] = push[t, 1, z] + near_buf[t, z]

        beside()

        for y in range(ROWS_Y + 1):
            for way, z in ((DOWN, 3), (UP, 1)):

                @pl.when(from_z[way])
                def _():
                    z_far_copy(t, way, y).wait_recv()
                    push[t, far, z, y] = push[t, far, z, y] + z_buf[t, way, 0, y]

                if y < ROWS_Y:

                    @pl.when(has_far)
                    def _():
                        far_copy(t, z, y).start()

        @pl.when(has_far)
        def _():
            corner_copy(t).start()

        for part in (0, 1):
            rows = slice(ROWS_Y, ROWS_Y + 1) if part == 0 else slice(0, ROWS_Y)
            for way, z in ((DOWN, 3), (UP, 1)):

                @pl.when(from_z[way])
                def _():
                    z_own_copy(t, way, part).wait_recv()
                    push[t, 1, z, rows] = push[t, 1, z, rows] + z_buf[t, way, 1, rows]

            if part == 0:
                y_copy(t).start()

        later()

        @pl.when(has_far)
        def _():
            middle_copy(t).wait_recv()
            push[t, 1, 2, :ROWS_Y] = push[t, 1, 2, :ROWS_Y] + far_buf[t, 1]
            for y in range(ROWS_Y):
                for z in (3, 1):
                    far_copy(t, z, y).wait_recv()
                    push[t, 1, z, y] = push[t, 1, z, y] + far_buf[t, z - 1, y]

        y_copy(t).wait_recv()
        for z in range(ROWS_Z):
            push[t, 1, z + 1, halo_row] = push[t, 1, z + 1, halo_row] + y_buf[t, z]

        @pl.when(has_far)
        def _():
            corner_copy(t).wait_recv()
            for z in range(ROWS_Z):
                push[t, 1, z + 1, halo_row] = push[t, 1, z + 1, halo_row] + corner_buf[t, z]

    def finish(t):
        for way in (UP, DOWN):

            @pl.when(has_z[way])
            def _():
                for y in range(ROWS_Y + 1):
                    z_far_copy(t, way, y).wait_send()
                for part in (0, 1):
                    z_own_copy(t, way, part).wait_send()

        for z in range(ROWS_Z + 2):
            near_copy(t, z).wait_send()

        @pl.when(has_far)
        def _():
            middle_copy(t).wait_send()
            corner_copy(t).wait_send()
            for y in range(ROWS_Y):
                for z in (3, 1):
                    far_copy(t, z, y).wait_send()

        y_copy(t).wait_send()

    cells = [(b, cz) for b in range(ROWS_Y) for cz in range(ROWS_Z)]

    def summed(terms):
        acc = None
        for term in terms:
            acc = term if acc is None else acc + term
        return jnp.sum(acc, axis=0, keepdims=True)

    stages = ((plane_buf, me1, peer1, steps1), (line_buf, me2, peer2, steps2))

    def exchange_start(t, stage):
        buf, me, peer, steps = stages[stage]
        for step in steps:
            send(
                buf.at[t, me], buf.at[t, me], gs.at[t, stage], gr.at[t, stage], peer(step)
            ).start()

    def exchange_end(t, stage):
        buf, me, peer, steps = stages[stage]
        every = buf.at[t, pl.ds(0, len(steps))]
        copy = send(every, every, gs.at[t, stage], gr.at[t, stage], peer(steps[0]))
        copy.wait_send()
        copy.wait_recv()
        return rows_of(buf[t])

    def put(buf, t, me, rows):
        blank = [jnp.zeros((1, RHS), jnp.float32)] * (8 - len(rows))
        buf[t, me] = jnp.concatenate(list(rows) + blank, axis=0)

    def first_sums():
        g = summed(field[b, cz] * field[b, cz] for b, cz in cells)
        a = summed(wide(0, b, cz) * field[b, cz] for b, cz in cells)
        c = divided(a, g)
        r = summed((wide(0, b, cz) - c * field[b, cz]) ** 2 for b, cz in cells)
        e = summed((wide(0, b, cz) - c * field[b, cz]) * field[b, cz] for b, cz in cells)
        put(plane_buf, 0, me1, (g, c, r, e))
        exchange_start(0, 0)

    def first_layer():
        rows = exchange_end(0, 0)
        put(line_buf, 0, me2, merged_one(*rows[:4])[:4])
        exchange_start(0, 1)

    def nothing():
        pass

    apply(0, nothing, nothing)
    apply(1, first_sums, first_layer)
    g, c, r, e, a = merged_one(*exchange_end(0, 1)[:4])
    scale_square = g / entries + epsilon
    scale = jnp.sqrt(scale_square)
    coef_one = a / entries / scale_square
    d = c - coef_one
    r = jnp.maximum(r + d * (2.0 * e + d * g), 0.0)
    norm_one = jnp.sqrt(r / entries / scale_square + epsilon)
    inv_scale = 1.0 / scale
    inv_second = 1.0 / norm_one
    for b, cz in cells:
        first = field[b, cz] * inv_scale
        wide_one = wide(0, b, cz) * inv_scale
        field[b, cz] = first
        second[b, cz] = (wide_one - coef_one * first) * inv_second
        image[b, cz] = (wide(1, b, cz) * inv_scale - coef_one * wide_one) * inv_second

    g11 = summed(field[b, cz] * field[b, cz] for b, cz in cells)
    g12 = summed(field[b, cz] * second[b, cz] for b, cz in cells)
    g22 = summed(second[b, cz] * second[b, cz] for b, cz in cells)
    a1 = summed(image[b, cz] * field[b, cz] for b, cz in cells)
    a2 = summed(image[b, cz] * second[b, cz] for b, cz in cells)
    c1, c2 = fitted(g11, g12, g22, a1, a2)
    for b, cz in cells:
        rest_ref[b, cz] = image[b, cz] - c1 * field[b, cz] - c2 * second[b, cz]
    r = summed(rest_ref[b, cz] * rest_ref[b, cz] for b, cz in cells)
    e1 = summed(rest_ref[b, cz] * field[b, cz] for b, cz in cells)
    e2 = summed(rest_ref[b, cz] * second[b, cz] for b, cz in cells)
    put(plane_buf, 1, me1, (g11, g12, g22, c1, c2, r, e1, e2))
    exchange_start(1, 0)
    put(line_buf, 1, me2, merged_two(*exchange_end(1, 0))[:8])
    exchange_start(1, 1)
    finish(0)
    finish(1)
    g11, g12, g22, c1, c2, r, e1, e2, a1, a2 = merged_two(*exchange_end(1, 1))
    coef_two = a1 / entries
    coef_three = a2 / entries
    d1, d2 = c1 - coef_two, c2 - coef_three
    p1 = d1 * g11 + d2 * g12
    p2 = d1 * g12 + d2 * g22
    r = jnp.maximum(r + d1 * (2.0 * e1 + p1) + d2 * (2.0 * e2 + p2), 0.0)
    norm_two = jnp.sqrt(r / entries + epsilon)
    for b, cz in cells:
        rest_ref[b, cz] = image[b, cz] - coef_two * field[b, cz] - coef_three * second[b, cz]
    hess_ref[...] = jnp.concatenate(
        [coef_one, norm_one, coef_two, coef_three, norm_two, norm_two, norm_two, norm_two], axis=0
    )


def per_device(nx, ny, nz, jacobian, columns, start, velocity, design, mask):
    n1 = nz * ny * 2
    n2 = nx // 2
    codes = jnp.transpose(columns, (0, 2, 1, 3)).reshape(ROWS_Z, ROWS_Y, SLOTS)
    block = (WIDTH, RHS)
    f32 = jnp.float32
    rest, hess = pl.pallas_call(
        functools.partial(kernel, nx, ny, nz),
        out_shape=(
            jax.ShapeDtypeStruct((ROWS_Y, ROWS_Z) + block, f32),
            jax.ShapeDtypeStruct((8, RHS), f32),
        ),
        in_specs=[
            pl.BlockSpec(memory_space=pltpu.VMEM),
            pl.BlockSpec(memory_space=pltpu.HBM),
            pl.BlockSpec(memory_space=pltpu.HBM),
        ],
        out_specs=(
            pl.BlockSpec(memory_space=pltpu.VMEM),
            pl.BlockSpec(memory_space=pltpu.VMEM),
        ),
        scratch_shapes=[
            pltpu.VMEM((16, 128), jnp.int32),
            pltpu.SMEM((16, 128), jnp.int32),
            pltpu.VMEM((ROWS_Z, ROWS_Y, WIDTH, SLOTS * WIDTH), jnp.bfloat16),
            pltpu.VMEM((ROWS_Z * ROWS_Y // 2, SLOTS * WIDTH, 4 * WIDTH), jnp.bfloat16),
            pltpu.VMEM((ROWS_Z, ROWS_Y, SLOTS) + block, f32),
            pltpu.VMEM((2, 3, ROWS_Z + 2, ROWS_Y + 1) + block, f32),
            pltpu.VMEM((2, ROWS_Z + 2, ROWS_Y + 1) + block, f32),
            pltpu.VMEM((2, 2, 2, ROWS_Y + 1) + block, f32),
            pltpu.VMEM((2, ROWS_Z, ROWS_Y) + block, f32),
            pltpu.VMEM((2, ROWS_Z) + block, f32),
            pltpu.VMEM((2, ROWS_Z) + block, f32),
            pltpu.VMEM((ROWS_Y, ROWS_Z) + block, f32),
            pltpu.VMEM((ROWS_Y, ROWS_Z) + block, f32),
            pltpu.VMEM((ROWS_Y, ROWS_Z) + block, f32),
            pltpu.VMEM((2, n1, 8, RHS), f32),
            pltpu.VMEM((2, n2, 8, RHS), f32),
            pltpu.SemaphoreType.DMA,
            pltpu.SemaphoreType.DMA((3,)),
            pltpu.SemaphoreType.DMA,
            pltpu.SemaphoreType.DMA((2, ROWS_Z + 2)),
            pltpu.SemaphoreType.DMA((2, ROWS_Z + 2)),
            pltpu.SemaphoreType.DMA((2, 2, ROWS_Y + 1)),
            pltpu.SemaphoreType.DMA((2, 2, ROWS_Y + 1)),
            pltpu.SemaphoreType.DMA((2, 2, 2)),
            pltpu.SemaphoreType.DMA((2, 2, 2)),
            pltpu.SemaphoreType.DMA((2,)),
            pltpu.SemaphoreType.DMA((2,)),
            pltpu.SemaphoreType.DMA((2, 2, ROWS_Y)),
            pltpu.SemaphoreType.DMA((2, 2, ROWS_Y)),
            pltpu.SemaphoreType.DMA((2,)),
            pltpu.SemaphoreType.DMA((2,)),
            pltpu.SemaphoreType.DMA((2,)),
            pltpu.SemaphoreType.DMA((2,)),
            pltpu.SemaphoreType.DMA((2, 2)),
            pltpu.SemaphoreType.DMA((2, 2)),
        ],
        compiler_params=pltpu.CompilerParams(
            collective_id=0, has_side_effects=True, vmem_limit_bytes=52 * 1024 * 1024
        ),
    )(
        codes,
        jacobian.reshape(ROWS_Y, ROWS_Z, WIDTH, SLOTS * WIDTH),
        start.reshape((ROWS_Y, ROWS_Z) + block),
    )
    hessenberg = hess[:5]
    adjoint = (rest / hess[4]).reshape(start.shape)
    cells = design.shape[3]
    shaped = adjoint.reshape(adjoint.shape[:3] + (WIDTH // cells, cells, RHS))
    dotted = jnp.sum(velocity[..., None] * shaped[:, :, :, 0:3], axis=3)
    slope = -0.11 / ((0.1 + design) * (0.1 + design))
    sensitivity = (mask.astype(f32) * slope)[..., None] * dotted
    return (adjoint, hessenberg, sensitivity)


def solution(mesh):
    shape = mesh.shape
    in_specs = (
        P("gx", "gy", "gz", None, None),
        P("gx", "gy", "gz", None),
        P("gx", "gy", "gz", None, None),
        P("gx", "gy", "gz", None, None),
        P("gx", "gy", "gz", None),
        P("gx", "gy", "gz", None),
    )
    out_specs = (P("gx", "gy", "gz", None, None), P(), P("gx", "gy", "gz", None, None))
    return jax.shard_map(
        functools.partial(per_device, shape["gx"], shape["gy"], shape["gz"]),
        mesh=mesh,
        in_specs=in_specs,
        out_specs=out_specs,
        check_vma=False,
    )
```

time: 84.8 us -> 57.8 us (0.68)
  Pallas kernels: 77.7 us -> 52.9 us
  local copies, waits for them, and re-layouts: 4.12 us -> 2.3 us
    pallas_call x1, Pallas kernels: 77.7 us -> 52.9 us  [per_device(): pl.pallas_call(functools.partial(kernel, nx, ny, nz), out_shape=(jax.Shap...]
    unnamed x12 -> x11, local copies, waits for them, and re-layouts: 4.09 us -> 2.28 us
where the time goes in v2:
time: 57.8 us; the launch traced here: 57.6 us
  Pallas kernels  52.9 us (92%)
  local copies, waits for them, and re-layouts  2.3 us (4%)
  other arithmetic  1.71 us (3%)
  between operations  0.72 us (1%)
    pallas_call x1, Pallas kernels, per_device(): pl.pallas_call(functools.partial(kernel, nx, ny, nz), out_shape=(jax.Shap...  52.9 us
    unnamed x11, local copies, waits for them, and re-layouts  2.28 us

profile of v2, /device:TPU:1, one launch (start us, length us, event | category | flops | bytes accessed | tf_op | source)
XLA Modules:
  0.0 57.6 jit_solution(16826490152119086192)
XLA Ops:
  0.6 0.0 copy-start
  0.6 1.0 %copy-done = f32[1,4,3,64,128]{4,3,2,1,0:T(8,128)S(1)} copy-done((f32[1,4,3,64,128]{4,3,2,1,0:T(8,128)S(1)}, f32[1,4,3,64,128]{4,3,2,1,0:T(8,128)}, u32[]{:S(2)}) %copy-start) | copy-done | bytes 393240
  1.6 0.0 copy-start.1
  1.6 0.7 %copy-done.1 = s32[1,4,3,27]{3,1,2,0:T(4,128)S(1)} copy-done((s32[1,4,3,27]{3,1,2,0:T(4,128)S(1)}, s32[1,4,3,27]{3,1,2,0:T(4,128)}, u32[]{:S(2)}) %copy-start.1) | copy-done | bytes 1320
  2.3 0.0 copy-start.2
  2.3 0.0 copy-start.3
  2.3 0.0 copy-start.4
  2.3 52.9 %shard_map.85 = (f32[4,3,64,128]{3,2,1,0:T(8,128)S(1)}, f32[8,128]{1,0:T(8,128)S(1)}) custom-call(s32[3,4,27]{2,1,0:T(4,128)S(1)} %bitcast.17, bf16[4,3,64,1728]{3,2,1,0:T(8,128)(2,1)} %bitcast.19, f32[4,3,64,128]{3,2,1,0:T(8,128)S(1)} %bitcast.16), custom_call_target="tpu_custom_call" | custom-call | tf_op jit(solution)/shard_map/pallas_call | solution.py:517
  55.3 0.0 copy-done.2
  55.3 0.1 fusion
  55.4 0.0 copy-done.3
  55.4 0.0 copy-done.4
  55.5 0.7 %bitcast_multiply_fusion = f32[1,4,3,16,128]{4,3,2,1,0:T(8,128)} fusion(f32[4,3,16,128]{3,2,1,0:T(8,128)S(1)} %fusion, f32[4,3,16]{2,1,0:T(4,128)S(1)} %copy.9), kind=kLoop, calls=%fused_computation.3 | loop fusion | flops 24576 | bytes 197376 | tf_op jit(solution)/shard_map/mul | solution.py:583
  56.2 0.8 %fusion.2 = f32[1,4,3,64,128]{4,3,2,1,0:T(8,128)} fusion(f32[4,3,64,128]{3,2,1,0:T(8,128)S(1)} %get-tuple-element.5, f32[128]{0:T(128)S(1)} %slice_bitcast_fusion), kind=kLoop, calls=%fused_computation.7 | loop fusion | flops 98304 | bytes 786944 | tf_op jit(solution)/shard_map/reshape | solution.py:578
  57.0 0.6 %copy.12 = f32[5,128]{1,0:T(8,128)} copy(f32[5,128]{1,0:T(8,128)S(1)} %bitcast.18) | data formatting | bytes 5120
  (5 shorter events, 0.1 us)
Async XLA Ops:
  0.6 1.0 %copy-start = (f32[1,4,3,64,128]{4,3,2,1,0:T(8,128)S(1)}, f32[1,4,3,64,128]{4,3,2,1,0:T(8,128)}, u32[]{:S(2)}) copy-start(f32[1,4,3,64,128]{4,3,2,1,0:T(8,128)} %param.8) | copy-start | bytes 1179652
  1.6 0.7 %copy-start.1 = (s32[1,4,3,27]{3,1,2,0:T(4,128)S(1)}, s32[1,4,3,27]{3,1,2,0:T(4,128)}, u32[]{:S(2)}) copy-start(s32[1,4,3,27]{3,1,2,0:T(4,128)} %param.7) | copy-start | bytes 3892
  2.3 52.9 %copy-start.2 = (f32[1,4,3,3,16]{4,1,3,2,0:T(4,128)S(1)}, f32[1,4,3,3,16]{4,1,3,2,0:T(4,128)}, u32[]{:S(2)}) copy-start(f32[1,4,3,3,16]{4,1,3,2,0:T(4,128)} %param.9) | copy-start | bytes 6916
  2.3 53.1 %copy-start.3 = (f32[1,4,3,16]{3,1,2,0:T(4,128)S(1)}, f32[1,4,3,16]{3,1,2,0:T(4,128)}, u32[]{:S(2)}) copy-start(f32[1,4,3,16]{3,1,2,0:T(4,128)} %param.10) | copy-start | bytes 2308
  2.3 53.1 %copy-start.4 = (s32[1,4,3,16]{3,1,2,0:T(4,128)S(1)}, s32[1,4,3,16]{3,1,2,0:T(4,128)}, u32[]{:S(2)}) copy-start(s32[1,4,3,16]{3,1,2,0:T(4,128)} %param.11) | copy-start | bytes 2308

commit v3 on v2

--- a/solution.py
+++ b/solution.py
@@ -69,17 +69,6 @@
     gy = lax.axis_index("gy")
     gz = lax.axis_index("gz")
     entries = float(nx * ny * nz * ROWS_Y * ROWS_Z * WIDTH)
-
-    field_copy = pltpu.make_async_copy(start_ref, field, ssem)
-
-    def j_copy(order, cz):
-        return pltpu.make_async_copy(j_ref.at[:, cz], jv.at[cz], jsem.at[order])
-
-    cz_order = (0, 2, 1)
-    j_copy(0, 0).start()
-    field_copy.start()
-    j_copy(1, 2).start()
-    j_copy(2, 1).start()
 
     layers = nx // 4
     layer = gx // 4
@@ -128,10 +117,11 @@
     def greet(device):
         pl.semaphore_signal(barrier, inc=1, device_id=device, device_id_type=MESH)
 
-    for step in steps1:
-        greet(peer1(step))
-    for step in steps2:
-        greet(peer2(step))
+    for k in range(max(len(steps1), len(steps2))):
+        if k < len(steps1):
+            greet(peer1(steps1[k]))
+        if k < len(steps2):
+            greet(peer2(steps2[k]))
 
     @pl.when(has_far)
     def _():
@@ -139,6 +129,17 @@
         greet(corner_device)
 
     greeted = n1 - 1 + n2 - 1 + jnp.where(has_far, 2, 0)
+
+    field_copy = pltpu.make_async_copy(start_ref, field, ssem)
+
+    def j_copy(order, cz):
+        return pltpu.make_async_copy(j_ref.at[:, cz], jv.at[cz], jsem.at[order])
+
+    cz_order = (0, 2, 1)
+    j_copy(0, 0).start()
+    field_copy.start()
+    j_copy(1, 2).start()
+    j_copy(2, 1).start()
 
     codes = jnp.concatenate([codes_ref[cz] for cz in range(ROWS_Z)], axis=0)
     place = lax.broadcasted_iota(jnp.int32, codes.shape, 1)
@@ -276,7 +277,7 @@
     def source(t, b, cz):
         return field[b, cz] if t == 0 else wide(0, b, cz)
 
-    def apply(t, beside, later):
+    def apply(t, beside, later, last):
         waiting = []
 
         def out(action):
@@ -285,10 +286,10 @@
             else:
                 action()
 
-        def out_z_far(way):
+        def out_z_far(way, rows=(0, ROWS_Y, 1)):
             @pl.when(has_z[way])
             def _():
-                for y in range(ROWS_Y + 1):
+                for y in rows:
                     z_far_copy(t, way, y).start()
 
         def out_middle():
@@ -323,6 +324,7 @@
             pl.semaphore_wait(barrier, greeted)
         for action in waiting:
             action()
+        beside()
         for way, z in ((DOWN, 0), (UP, 4)):
             near_copy(t, z).wait_recv()
             push[t, 1, z] = push[t, 1, z] + near_buf[t, z]
@@ -330,15 +332,19 @@
             @pl.when(has_z[way])
             def _():
                 z_own_copy(t, way, 0).start()
+
+        for way in (DOWN, UP):
+            out_z_far(way, (2, 3))
+
+            @pl.when(has_z[way])
+            def _():
                 z_own_copy(t, way, 1).start()
 
         for z in (2, 3, 1):
             near_copy(t, z).wait_recv()
             push[t, 1, z] = push[t, 1, z] + near_buf[t, z]
 
-        beside()
-
-        for y in range(ROWS_Y + 1):
+        def from_z_far(y):
             for way, z in ((DOWN, 3), (UP, 1)):
 
                 @pl.when(from_z[way])
@@ -352,11 +358,7 @@
                     def _():
                         far_copy(t, z, y).start()
 
-        @pl.when(has_far)
-        def _():
-            corner_copy(t).start()
-
-        for part in (0, 1):
+        def from_z_own(part):
             rows = slice(ROWS_Y, ROWS_Y + 1) if part == 0 else slice(0, ROWS_Y)
             for way, z in ((DOWN, 3), (UP, 1)):
 
@@ -365,29 +367,48 @@
                     z_own_copy(t, way, part).wait_recv()
                     push[t, 1, z, rows] = push[t, 1, z, rows] + z_buf[t, way, 1, rows]
 
-            if part == 0:
-                y_copy(t).start()
-
+        def from_far(y):
+            @pl.when(has_far)
+            def _():
+                for z in (3, 1):
+                    far_copy(t, z, y).wait_recv()
+                    push[t, 1, z, y] = push[t, 1, z, y] + far_buf[t, z - 1, y]
+
+        from_z_far(0)
+        from_z_far(ROWS_Y)
+
+        @pl.when(has_far)
+        def _():
+            corner_copy(t).start()
+
+        from_z_far(1)
+        from_z_own(0)
+        y_copy(t).start()
+        from_z_far(2)
+        from_z_far(3)
         later()
+        from_z_own(1)
 
         @pl.when(has_far)
         def _():
             middle_copy(t).wait_recv()
             push[t, 1, 2, :ROWS_Y] = push[t, 1, 2, :ROWS_Y] + far_buf[t, 1]
-            for y in range(ROWS_Y):
-                for z in (3, 1):
-                    far_copy(t, z, y).wait_recv()
-                    push[t, 1, z, y] = push[t, 1, z, y] + far_buf[t, z - 1, y]
-
-        y_copy(t).wait_recv()
-        for z in range(ROWS_Z):
-            push[t, 1, z + 1, halo_row] = push[t, 1, z + 1, halo_row] + y_buf[t, z]
+
+        from_far(0)
 
         @pl.when(has_far)
         def _():
             corner_copy(t).wait_recv()
             for z in range(ROWS_Z):
                 push[t, 1, z + 1, halo_row] = push[t, 1, z + 1, halo_row] + corner_buf[t, z]
+
+        from_far(1)
+        y_copy(t).wait_recv()
+        for z in range(ROWS_Z):
+            push[t, 1, z + 1, halo_row] = push[t, 1, z + 1, halo_row] + y_buf[t, z]
+        from_far(2)
+        last()
+        from_far(3)
 
     def finish(t):
         for way in (UP, DOWN):
@@ -458,27 +479,36 @@
     def nothing():
         pass
 
-    apply(0, nothing, nothing)
-    apply(1, first_sums, first_layer)
-    g, c, r, e, a = merged_one(*exchange_end(0, 1)[:4])
-    scale_square = g / entries + epsilon
-    scale = jnp.sqrt(scale_square)
-    coef_one = a / entries / scale_square
-    d = c - coef_one
-    r = jnp.maximum(r + d * (2.0 * e + d * g), 0.0)
-    norm_one = jnp.sqrt(r / entries / scale_square + epsilon)
-    inv_scale = 1.0 / scale
-    inv_second = 1.0 / norm_one
+    found = []
+
+    def first_end():
+        g, c, r, e, a = merged_one(*exchange_end(0, 1)[:4])
+        scale_square = g / entries + epsilon
+        coef_one = a / entries / scale_square
+        d = c - coef_one
+        r = jnp.maximum(r + d * (2.0 * e + d * g), 0.0)
+        norm_one = jnp.sqrt(r / entries / scale_square + epsilon)
+        inv_scale = 1.0 / jnp.sqrt(scale_square)
+        inv_second = 1.0 / norm_one
+        for b, cz in cells:
+            first = field[b, cz] * inv_scale
+            wide_one = wide(0, b, cz) * inv_scale
+            field[b, cz] = first
+            second[b, cz] = (wide_one - coef_one * first) * inv_second
+        g11 = summed(field[b, cz] * field[b, cz] for b, cz in cells)
+        g12 = summed(field[b, cz] * second[b, cz] for b, cz in cells)
+        g22 = summed(second[b, cz] * second[b, cz] for b, cz in cells)
+        found.extend(
+            (coef_one, norm_one, inv_scale * inv_second, coef_one * inv_scale * inv_second)
+        )
+        found.extend((g11, g12, g22))
+
+    apply(0, nothing, nothing, nothing)
+    apply(1, first_sums, first_layer, first_end)
+    coef_one, norm_one, gain, shift, g11, g12, g22 = found
+
     for b, cz in cells:
-        first = field[b, cz] * inv_scale
-        wide_one = wide(0, b, cz) * inv_scale
-        field[b, cz] = first
-        second[b, cz] = (wide_one - coef_one * first) * inv_second
-        image[b, cz] = (wide(1, b, cz) * inv_scale - coef_one * wide_one) * inv_second
-
-    g11 = summed(field[b, cz] * field[b, cz] for b, cz in cells)
-    g12 = summed(field[b, cz] * second[b, cz] for b, cz in cells)
-    g22 = summed(second[b, cz] * second[b, cz] for b, cz in cells)
+        image[b, cz] = wide(1, b, cz) * gain - wide(0, b, cz) * shift
     a1 = summed(image[b, cz] * field[b, cz] for b, cz in cells)
     a2 = summed(image[b, cz] * second[b, cz] for b, cz in cells)
     c1, c2 = fitted(g11, g12, g22, a1, a2)

time: 57.8 us -> 55.2 us (0.955)
  Pallas kernels: 52.9 us -> 50.3 us
    pallas_call x1, Pallas kernels: 52.9 us -> 50.3 us  [per_device(): pl.pallas_call(functools.partial(kernel, nx, ny, nz), out_shape=(jax.Shap...]
where the time goes in v3:
time: 55.2 us; the launch traced here: 55 us
  Pallas kernels  50.3 us (91%)
  local copies, waits for them, and re-layouts  2.3 us (4%)
  other arithmetic  1.71 us (3%)
  between operations  0.72 us (1%)
    pallas_call x1, Pallas kernels, per_device(): pl.pallas_call(functools.partial(kernel, nx, ny, nz), out_shape=(jax.Shap...  50.3 us
    unnamed x11, local copies, waits for them, and re-layouts  2.28 us

profile of v3, /device:TPU:1, one launch (start us, length us, event | category | flops | bytes accessed | tf_op | source)
XLA Modules:
  0.0 55.0 jit_solution(13996360077033538301)
XLA Ops:
  0.6 0.0 copy-start
  0.6 1.0 %copy-done = f32[1,4,3,64,128]{4,3,2,1,0:T(8,128)S(1)} copy-done((f32[1,4,3,64,128]{4,3,2,1,0:T(8,128)S(1)}, f32[1,4,3,64,128]{4,3,2,1,0:T(8,128)}, u32[]{:S(2)}) %copy-start) | copy-done | bytes 393240
  1.6 0.0 copy-start.1
  1.6 0.7 %copy-done.1 = s32[1,4,3,27]{3,1,2,0:T(4,128)S(1)} copy-done((s32[1,4,3,27]{3,1,2,0:T(4,128)S(1)}, s32[1,4,3,27]{3,1,2,0:T(4,128)}, u32[]{:S(2)}) %copy-start.1) | copy-done | bytes 1320
  2.3 0.0 copy-start.2
  2.3 0.0 copy-start.3
  2.3 0.0 copy-start.4
  2.3 50.3 %shard_map.85 = (f32[4,3,64,128]{3,2,1,0:T(8,128)S(1)}, f32[8,128]{1,0:T(8,128)S(1)}) custom-call(s32[3,4,27]{2,1,0:T(4,128)S(1)} %bitcast.17, bf16[4,3,64,1728]{3,2,1,0:T(8,128)(2,1)} %bitcast.19, f32[4,3,64,128]{3,2,1,0:T(8,128)S(1)} %bitcast.16), custom_call_target="tpu_custom_call" | custom-call | tf_op jit(solution)/shard_map/pallas_call | solution.py:547
  52.7 0.0 copy-done.2
  52.7 0.1 fusion
  52.9 0.0 copy-done.3
  52.9 0.0 copy-done.4
  52.9 0.7 %bitcast_multiply_fusion = f32[1,4,3,16,128]{4,3,2,1,0:T(8,128)} fusion(f32[4,3,16,128]{3,2,1,0:T(8,128)S(1)} %fusion, f32[4,3,16]{2,1,0:T(4,128)S(1)} %copy.9), kind=kLoop, calls=%fused_computation.3 | loop fusion | flops 24576 | bytes 197376 | tf_op jit(solution)/shard_map/mul | solution.py:613
  53.7 0.8 %fusion.2 = f32[1,4,3,64,128]{4,3,2,1,0:T(8,128)} fusion(f32[4,3,64,128]{3,2,1,0:T(8,128)S(1)} %get-tuple-element.5, f32[128]{0:T(128)S(1)} %slice_bitcast_fusion), kind=kLoop, calls=%fused_computation.7 | loop fusion | flops 98304 | bytes 786944 | tf_op jit(solution)/shard_map/reshape | solution.py:608
  54.5 0.6 %copy.12 = f32[5,128]{1,0:T(8,128)} copy(f32[5,128]{1,0:T(8,128)S(1)} %bitcast.18) | data formatting | bytes 5120
  (5 shorter events, 0.1 us)
Async XLA Ops:
  0.6 1.0 %copy-start = (f32[1,4,3,64,128]{4,3,2,1,0:T(8,128)S(1)}, f32[1,4,3,64,128]{4,3,2,1,0:T(8,128)}, u32[]{:S(2)}) copy-start(f32[1,4,3,64,128]{4,3,2,1,0:T(8,128)} %param.8) | copy-start | bytes 1179652
  1.6 0.7 %copy-start.1 = (s32[1,4,3,27]{3,1,2,0:T(4,128)S(1)}, s32[1,4,3,27]{3,1,2,0:T(4,128)}, u32[]{:S(2)}) copy-start(s32[1,4,3,27]{3,1,2,0:T(4,128)} %param.7) | copy-start | bytes 3892
  2.3 50.4 %copy-start.2 = (f32[1,4,3,3,16]{4,1,3,2,0:T(4,128)S(1)}, f32[1,4,3,3,16]{4,1,3,2,0:T(4,128)}, u32[]{:S(2)}) copy-start(f32[1,4,3,3,16]{4,1,3,2,0:T(4,128)} %param.9) | copy-start | bytes 6916
  2.3 50.6 %copy-start.3 = (f32[1,4,3,16]{3,1,2,0:T(4,128)S(1)}, f32[1,4,3,16]{3,1,2,0:T(4,128)}, u32[]{:S(2)}) copy-start(f32[1,4,3,16]{3,1,2,0:T(4,128)} %param.10) | copy-start | bytes 2308
  2.3 50.6 %copy-start.4 = (s32[1,4,3,16]{3,1,2,0:T(4,128)S(1)}, s32[1,4,3,16]{3,1,2,0:T(4,128)}, u32[]{:S(2)}) copy-start(s32[1,4,3,16]{3,1,2,0:T(4,128)} %param.11) | copy-start | bytes 2308

commit v4 on v3

--- a/solution.py
+++ b/solution.py
@@ -60,10 +60,10 @@
 
 def kernel(
     nx, ny, nz,
-    codes_ref, j_ref, start_ref,
+    codes_hbm, j_ref, start_ref,
     rest_ref, hess_ref,
-    inv_vmem, inv_ref, jv, jt, prod, push, near_buf, z_buf, far_buf, corner_buf, y_buf, field, second, image, plane_buf, line_buf,
-    isem, jsem, ssem, ns, nr, zs, zr, zos, zor, ms, mr, fs, fr, cs, cr, ys, yr, gs, gr,
+    codes_ref, inv_vmem, inv_ref, jv, jt, prod, push, near_buf, z_buf, far_buf, corner_buf, y_buf, field, second, image, plane_buf, line_buf,
+    csem, isem, jsem, ssem, ns, nr, zs, zr, zos, zor, ms, mr, fs, fr, cs, cr, ys, yr, gs, gr,
 ):
     gx = lax.axis_index("gx")
     gy = lax.axis_index("gy")
@@ -136,11 +136,14 @@
         return pltpu.make_async_copy(j_ref.at[:, cz], jv.at[cz], jsem.at[order])
 
     cz_order = (0, 2, 1)
+    codes_copy = pltpu.make_async_copy(codes_hbm, codes_ref, csem)
+    codes_copy.start()
     j_copy(0, 0).start()
     field_copy.start()
     j_copy(1, 2).start()
     j_copy(2, 1).start()
 
+    codes_copy.wait()
     codes = jnp.concatenate([codes_ref[cz] for cz in range(ROWS_Z)], axis=0)
     place = lax.broadcasted_iota(jnp.int32, codes.shape, 1)
     inverse = jnp.zeros_like(codes)
@@ -278,13 +281,13 @@
         return field[b, cz] if t == 0 else wide(0, b, cz)
 
     def apply(t, beside, later, last):
-        waiting = []
+        met = []
 
         def out(action):
-            if t == 0:
-                waiting.append(action)
-            else:
-                action()
+            if t == 0 and not met:
+                met.append(True)
+                pl.semaphore_wait(barrier, greeted)
+            action()
 
         def out_z_far(way, rows=(0, ROWS_Y, 1)):
             @pl.when(has_z[way])
@@ -297,6 +300,8 @@
             def _():
                 middle_copy(t).start()
 
+        if t == 1:
+            beside()
         for order, cz in enumerate(cz_order):
             if t == 0:
                 j_copy(order, cz).wait()
@@ -320,11 +325,6 @@
         gather_plane(t, far, 1)
         for z in (0, 4, 2, 3, 1):
             gather_plane(t, 1, z)
-        if t == 0:
-            pl.semaphore_wait(barrier, greeted)
-        for action in waiting:
-            action()
-        beside()
         for way, z in ((DOWN, 0), (UP, 4)):
             near_copy(t, z).wait_recv()
             push[t, 1, z] = push[t, 1, z] + near_buf[t, z]
@@ -340,6 +340,8 @@
             def _():
                 z_own_copy(t, way, 1).start()
 
+        if t == 0:
+            beside()
         for z in (2, 3, 1):
             near_copy(t, z).wait_recv()
             push[t, 1, z] = push[t, 1, z] + near_buf[t, z]
@@ -462,8 +464,13 @@
         blank = [jnp.zeros((1, RHS), jnp.float32)] * (8 - len(rows))
         buf[t, me] = jnp.concatenate(list(rows) + blank, axis=0)
 
+    squares = []
+
+    def first_squares():
+        squares.append(summed(field[b, cz] * field[b, cz] for b, cz in cells))
+
     def first_sums():
-        g = summed(field[b, cz] * field[b, cz] for b, cz in cells)
+        g = squares[0]
         a = summed(wide(0, b, cz) * field[b, cz] for b, cz in cells)
         c = divided(a, g)
         r = summed((wide(0, b, cz) - c * field[b, cz]) ** 2 for b, cz in cells)
@@ -503,7 +510,7 @@
         )
         found.extend((g11, g12, g22))
 
-    apply(0, nothing, nothing, nothing)
+    apply(0, first_squares, nothing, nothing)
     apply(1, first_sums, first_layer, first_end)
     coef_one, norm_one, gain, shift, g11, g12, g22 = found
 
@@ -551,7 +558,7 @@
             jax.ShapeDtypeStruct((8, RHS), f32),
         ),
         in_specs=[
-            pl.BlockSpec(memory_space=pltpu.VMEM),
+            pl.BlockSpec(memory_space=pltpu.HBM),
             pl.BlockSpec(memory_space=pltpu.HBM),
             pl.BlockSpec(memory_space=pltpu.HBM),
         ],
@@ -560,6 +567,7 @@
             pl.BlockSpec(memory_space=pltpu.VMEM),
         ),
         scratch_shapes=[
+            pltpu.VMEM((ROWS_Z, ROWS_Y, SLOTS), jnp.int32),
             pltpu.VMEM((16, 128), jnp.int32),
             pltpu.SMEM((16, 128), jnp.int32),
             pltpu.VMEM((ROWS_Z, ROWS_Y, WIDTH, SLOTS * WIDTH), jnp.bfloat16),
@@ -576,6 +584,7 @@
             pltpu.VMEM((ROWS_Y, ROWS_Z) + block, f32),
             pltpu.VMEM((2, n1, 8, RHS), f32),
             pltpu.VMEM((2, n2, 8, RHS), f32),
+            pltpu.SemaphoreType.DMA,
             pltpu.SemaphoreType.DMA,
             pltpu.SemaphoreType.DMA((3,)),
             pltpu.SemaphoreType.DMA,
@@ -600,9 +609,9 @@
             collective_id=0, has_side_effects=True, vmem_limit_bytes=52 * 1024 * 1024
         ),
     )(
-        codes,
+        pltpu.with_memory_space_constraint(codes, pltpu.HBM),
         jacobian.reshape(ROWS_Y, ROWS_Z, WIDTH, SLOTS * WIDTH),
-        start.reshape((ROWS_Y, ROWS_Z) + block),
+        pltpu.with_memory_space_constraint(start.reshape((ROWS_Y, ROWS_Z) + block), pltpu.HBM),
     )
     hessenberg = hess[:5]
     adjoint = (rest / hess[4]).reshape(start.shape)

time: 55.2 us -> 53.6 us (0.971)
  local copies, waits for them, and re-layouts: 2.3 us -> 0.62 us
    unnamed x11 -> x7, local copies, waits for them, and re-layouts: 2.28 us -> 0.6 us
where the time goes in v4:
time: 53.6 us; the launch traced here: 53.5 us
  Pallas kernels  50.4 us (94%)
  other arithmetic  1.71 us (3%)
  between operations  0.73 us (1%)
  local copies, waits for them, and re-layouts  0.62 us (1%)
    pallas_call x1, Pallas kernels, per_device(): pl.pallas_call(functools.partial(kernel, nx, ny, nz), out_shape=(jax.Shap...  50.4 us

profile of v4, /device:TPU:1, one launch (start us, length us, event | category | flops | bytes accessed | tf_op | source)
XLA Modules:
  0.0 53.5 jit_solution(16290634447087984737)
XLA Ops:
  0.6 0.0 copy-start
  0.6 0.0 copy-start.1
  0.7 0.0 copy-start.2
  0.7 50.4 %shard_map.85 = (f32[4,3,64,128]{3,2,1,0:T(8,128)S(1)}, f32[8,128]{1,0:T(8,128)S(1)}) custom-call(s32[3,4,27]{2,1,0:T(4,128)} %bitcast.21, bf16[4,3,64,1728]{3,2,1,0:T(8,128)(2,1)} %bitcast.17, f32[4,3,64,128]{3,2,1,0:T(8,128)} %bitcast.19), custom_call_target="tpu_custom_call" | custom-call | tf_op jit(solution)/shard_map/pallas_call | solution.py:554
  51.1 0.0 copy-done
  51.2 0.1 fusion
  51.3 0.0 copy-done.1
  51.3 0.0 copy-done.2
  51.3 0.7 %bitcast_multiply_fusion = f32[1,4,3,16,128]{4,3,2,1,0:T(8,128)} fusion(f32[4,3,16,128]{3,2,1,0:T(8,128)S(1)} %fusion, f32[4,3,16]{2,1,0:T(4,128)S(1)} %copy.9), kind=kLoop, calls=%fused_computation.3 | loop fusion | flops 24576 | bytes 197376 | tf_op jit(solution)/shard_map/mul | solution.py:622
  52.1 0.8 %fusion.2 = f32[1,4,3,64,128]{4,3,2,1,0:T(8,128)} fusion(f32[4,3,64,128]{3,2,1,0:T(8,128)S(1)} %get-tuple-element.5, f32[128]{0:T(128)S(1)} %slice_bitcast_fusion), kind=kLoop, calls=%fused_computation.7 | loop fusion | flops 98304 | bytes 786944 | tf_op jit(solution)/shard_map/reshape | solution.py:617
  52.9 0.6 %copy.12 = f32[5,128]{1,0:T(8,128)} copy(f32[5,128]{1,0:T(8,128)S(1)} %bitcast.16) | data formatting | bytes 5120
  (5 shorter events, 0.1 us)
Async XLA Ops:
  0.6 50.5 %copy-start = (f32[1,4,3,3,16]{4,1,3,2,0:T(4,128)S(1)}, f32[1,4,3,3,16]{4,1,3,2,0:T(4,128)}, u32[]{:S(2)}) copy-start(f32[1,4,3,3,16]{4,1,3,2,0:T(4,128)} %param.9) | copy-start | bytes 6916
  0.6 50.7 %copy-start.1 = (f32[1,4,3,16]{3,1,2,0:T(4,128)S(1)}, f32[1,4,3,16]{3,1,2,0:T(4,128)}, u32[]{:S(2)}) copy-start(f32[1,4,3,16]{3,1,2,0:T(4,128)} %param.10) | copy-start | bytes 2308
  0.7 50.7 %copy-start.2 = (s32[1,4,3,16]{3,1,2,0:T(4,128)S(1)}, s32[1,4,3,16]{3,1,2,0:T(4,128)}, u32[]{:S(2)}) copy-start(s32[1,4,3,16]{3,1,2,0:T(4,128)} %param.11) | copy-start | bytes 2308

commit v5 on v4

--- a/solution.py
+++ b/solution.py
@@ -387,8 +387,8 @@
         from_z_own(0)
         y_copy(t).start()
         from_z_far(2)
+        later()
         from_z_far(3)
-        later()
         from_z_own(1)
 
         @pl.when(has_far)
@@ -452,13 +452,14 @@
                 buf.at[t, me], buf.at[t, me], gs.at[t, stage], gr.at[t, stage], peer(step)
             ).start()
 
-    def exchange_end(t, stage):
+    def exchange_whole(t, stage):
         buf, me, peer, steps = stages[stage]
         every = buf.at[t, pl.ds(0, len(steps))]
-        copy = send(every, every, gs.at[t, stage], gr.at[t, stage], peer(steps[0]))
-        copy.wait_send()
-        copy.wait_recv()
-        return rows_of(buf[t])
+        return send(every, every, gs.at[t, stage], gr.at[t, stage], peer(steps[0]))
+
+    def exchange_end(t, stage):
+        exchange_whole(t, stage).wait_recv()
+        return rows_of(stages[stage][0][t])
 
     def put(buf, t, me, rows):
         blank = [jnp.zeros((1, RHS), jnp.float32)] * (8 - len(rows))
@@ -530,6 +531,8 @@
     exchange_start(1, 1)
     finish(0)
     finish(1)
+    for t, stage in ((0, 0), (0, 1), (1, 0)):
+        exchange_whole(t, stage).wait_send()
     g11, g12, g22, c1, c2, r, e1, e2, a1, a2 = merged_two(*exchange_end(1, 1))
     coef_two = a1 / entries
     coef_three = a2 / entries
@@ -543,6 +546,7 @@
     hess_ref[...] = jnp.concatenate(
         [coef_one, norm_one, coef_two, coef_three, norm_two, norm_two, norm_two, norm_two], axis=0
     )
+    exchange_whole(1, 1).wait_send()
 
 
 def per_device(nx, ny, nz, jacobian, columns, start, velocity, design, mask):

time: 53.6 us -> 53.6 us (level)
  no operation moved by 1% of the time
where the time goes in v5:
time: 53.6 us; the launch traced here: 53.5 us
  Pallas kernels  50.4 us (94%)
  other arithmetic  1.71 us (3%)
  between operations  0.73 us (1%)
  local copies, waits for them, and re-layouts  0.62 us (1%)
    pallas_call x1, Pallas kernels, per_device(): pl.pallas_call(functools.partial(kernel, nx, ny, nz), out_shape=(jax.Shap...  50.4 us

profile of v5, /device:TPU:1, one launch (start us, length us, event | category | flops | bytes accessed | tf_op | source)
XLA Modules:
  0.0 53.5 jit_solution(15260782642805343990)
XLA Ops:
  0.6 0.0 copy-start
  0.6 0.0 copy-start.1
  0.7 0.0 copy-start.2
  0.7 50.4 %shard_map.85 = (f32[4,3,64,128]{3,2,1,0:T(8,128)S(1)}, f32[8,128]{1,0:T(8,128)S(1)}) custom-call(s32[3,4,27]{2,1,0:T(4,128)} %bitcast.21, bf16[4,3,64,1728]{3,2,1,0:T(8,128)(2,1)} %bitcast.17, f32[4,3,64,128]{3,2,1,0:T(8,128)} %bitcast.19), custom_call_target="tpu_custom_call" | custom-call | tf_op jit(solution)/shard_map/pallas_call | solution.py:558
  51.2 0.0 copy-done
  51.2 0.1 fusion
  51.3 0.0 copy-done.1
  51.3 0.0 copy-done.2
  51.4 0.7 %bitcast_multiply_fusion = f32[1,4,3,16,128]{4,3,2,1,0:T(8,128)} fusion(f32[4,3,16,128]{3,2,1,0:T(8,128)S(1)} %fusion, f32[4,3,16]{2,1,0:T(4,128)S(1)} %copy.9), kind=kLoop, calls=%fused_computation.3 | loop fusion | flops 24576 | bytes 197376 | tf_op jit(solution)/shard_map/mul | solution.py:626
  52.1 0.8 %fusion.2 = f32[1,4,3,64,128]{4,3,2,1,0:T(8,128)} fusion(f32[4,3,64,128]{3,2,1,0:T(8,128)S(1)} %get-tuple-element.5, f32[128]{0:T(128)S(1)} %slice_bitcast_fusion), kind=kLoop, calls=%fused_computation.7 | loop fusion | flops 98304 | bytes 786944 | tf_op jit(solution)/shard_map/reshape | solution.py:621
  52.9 0.6 %copy.12 = f32[5,128]{1,0:T(8,128)} copy(f32[5,128]{1,0:T(8,128)S(1)} %bitcast.16) | data formatting | bytes 5120
  (5 shorter events, 0.1 us)
Async XLA Ops:
  0.6 50.5 %copy-start = (f32[1,4,3,3,16]{4,1,3,2,0:T(4,128)S(1)}, f32[1,4,3,3,16]{4,1,3,2,0:T(4,128)}, u32[]{:S(2)}) copy-start(f32[1,4,3,3,16]{4,1,3,2,0:T(4,128)} %param.9) | copy-start | bytes 6916
  0.6 50.7 %copy-start.1 = (f32[1,4,3,16]{3,1,2,0:T(4,128)S(1)}, f32[1,4,3,16]{3,1,2,0:T(4,128)}, u32[]{:S(2)}) copy-start(f32[1,4,3,16]{3,1,2,0:T(4,128)} %param.10) | copy-start | bytes 2308
  0.7 50.7 %copy-start.2 = (s32[1,4,3,16]{3,1,2,0:T(4,128)S(1)}, s32[1,4,3,16]{3,1,2,0:T(4,128)}, u32[]{:S(2)}) copy-start(s32[1,4,3,16]{3,1,2,0:T(4,128)} %param.11) | copy-start | bytes 2308
